TPU v7x, 128 devices: a whole 4x4x4 slice. The times are simulated.
128 devices in a mesh: row: 8 (over z, core), col: 16 (over y, x).
Axes of the slice: x: 4, y: 4, z: 4, core: 2. Of those that a mesh axis runs over, the one named last changes fastest.
Arguments:
- atoms: bfloat16 [32768, 128], P(('row', 'col')), may hold values from -6 to 6
- atom_bias: bfloat16 [32768, 4, 128], P(('row', 'col')), may hold values from -10 to 400
- key_mask: int32 [1024, 128], P(('row', 'col')), may hold values 0 or 1
- atom_token: int32 [32768], P(('row', 'col')), may hold values from 0 to 4095, as said below
- tokens: bfloat16 [4096, 768], P('row'), may hold values from -6 to 6
- pair_bias: bfloat16 [16, 4096, 4096], P(None, 'row', 'col'), may hold values from -10 to 400
- token_mask: int32 [4096], P('col'), may hold values from 0 to 1, as said below
- atom_query: bfloat16 [128, 128], replicated, may hold values from -0.5 to 0.5
- atom_keyval: bfloat16 [128, 256], replicated, may hold values from -0.5 to 0.5
- atom_gate: bfloat16 [128, 128], replicated, may hold values from -0.5 to 0.5
- atom_out: bfloat16 [128, 128], replicated, may hold values from -0.5 to 0.5
- pool_weight: bfloat16 [128, 768], replicated, may hold values from -0.5 to 0.5
- token_query: bfloat16 [768, 768], replicated, may hold values from -0.21875 to 0.21875
- token_keyval: bfloat16 [768, 1536], replicated, may hold values from -0.21875 to 0.21875
- token_gate: bfloat16 [768, 768], replicated, may hold values from -0.21875 to 0.21875
- token_out: bfloat16 [768, 768], replicated, may hold values from -0.21875 to 0.21875
- trans_gate: bfloat16 [768, 1536], replicated, may hold values from -0.21875 to 0.21875
- trans_up: bfloat16 [768, 1536], replicated, may hold values from -0.21875 to 0.21875
- trans_down: bfloat16 [1536, 768], replicated, may hold values from -0.15625 to 0.15625
- back_weight: bfloat16 [768, 128], replicated, may hold values from -0.21875 to 0.21875
Outputs:
- atoms_new: bfloat16 [32768, 128], P(('row', 'col'))
- tokens_new: bfloat16 [4096, 768], P('row')
Inputs may be any that keep to these rules, and one draw needn't show every extreme that they name: atom_token never falls along the atoms; the atoms of block r of 4096 atoms name exactly the tokens of block r of 512 tokens, each at least once. `token_mask`: 1 on a prefix of 2048 tokens or more, 0 after it; the last token is 0.
All inputs are finite; a program needn't handle non-finite values. No bound on the sum of `key_mask` on one device may be relied on, other than what follows from the above.
Results may differ from a plain program's by a relative error of at most 0.013.
Values may be sent and summed in bfloat16 or wider, within the bound.
A program may use at most 128 MiB of HBM per device.

v0:
```python
import jax
import jax.numpy as jnp
from jax import lax
from jax.sharding import PartitionSpec as P

HA = 4
DA = 32
WQ = 32
WK = 128
HT = 16
DT = 48


EPSILON = 1e-05
MASKED = -1000000000.0


def padded_2(x, sides, width):
    for axis, dim in sides:
        peers, length = (lax.axis_size(axis), x.shape[dim])
        up = [(i, (i + 1) % peers) for i in range(peers - 1)]
        down = [(j, i) for i, j in up]
        last = lax.slice_in_dim(x, length - width, length, axis=dim)
        initial = lax.slice_in_dim(x, 0, width, axis=dim)
        before = lax.ppermute(last, axis, up)
        after = lax.ppermute(initial, axis, down)
        x = jnp.concatenate([before, x, after], axis=dim)
    return x


def combined_all(x, axis, combine):
    everything = jax.tree.map(lambda part: lax.all_gather(part, axis), x)
    initial = jax.tree.map(lambda part: part[0], everything)

    def hop(k, so_far):
        return combine(so_far, jax.tree.map(lambda part: part[k], everything))

    return lax.fori_loop(1, lax.axis_size(axis), hop, initial)


def normalize(values):
    average = jnp.mean(values, axis=-1, keepdims=True)
    centred = values - average
    variance = jnp.mean(centred * centred, axis=-1, keepdims=True)
    return centred * lax.rsqrt(variance + EPSILON)


def product(left, right):
    return jnp.dot(left, right, preferred_element_type=jnp.float32)


def transition(rows_in, trans_gate, trans_up, trans_down):
    trans_norm = normalize(rows_in.astype(jnp.float32)).astype(jnp.bfloat16)
    trans_hidden = (
        jax.nn.silu(product(trans_norm, trans_gate)) * product(trans_norm, trans_up)
    ).astype(jnp.bfloat16)
    return (rows_in.astype(jnp.float32) + product(trans_hidden, trans_down)).astype(jnp.bfloat16)


def finish_rows(attended_rows, norm_rows, mid_rows, token_gate, token_out):
    gated = (attended_rows * jax.nn.sigmoid(product(norm_rows, token_gate))).astype(jnp.bfloat16)
    return (mid_rows.astype(jnp.float32) + product(gated, token_out)).astype(jnp.bfloat16)


def combine_parts(first, second):
    top_first, total_first, acc_first = first
    top_second, total_second, acc_second = second
    top_both = jnp.maximum(top_first, top_second)
    factor_first = jnp.exp(top_first - top_both)
    factor_second = jnp.exp(top_second - top_both)
    total_both = total_first * factor_first + total_second * factor_second
    row_count, head_count = top_first.shape
    acc_both = acc_first.reshape(row_count, head_count, -1) * factor_first[:, :, None]
    acc_both = acc_both + acc_second.reshape(row_count, head_count, -1) * factor_second[:, :, None]
    return (top_both, total_both, acc_both.reshape(acc_first.shape))


def on_device(
    atoms,
    atom_bias,
    key_mask,
    atom_token,
    tokens,
    pair_bias,
    token_mask,
    atom_query,
    atom_keyval,
    atom_gate,
    atom_out,
    pool_weight,
    token_query,
    token_keyval,
    token_gate,
    token_out,
    trans_gate,
    trans_up,
    trans_down,
    back_weight,
):
    atom_rows, atom_width = atoms.shape
    windows = atom_rows // WQ
    reach = (WK - WQ) // 2
    atom_norm = normalize(atoms.astype(jnp.float32)).astype(jnp.bfloat16)
    atom_queries = product(atom_norm, atom_query).astype(jnp.bfloat16)
    atom_kv = product(atom_norm, atom_keyval).astype(jnp.bfloat16)
    padded = padded_2(atom_kv, ((("row", "col"), 0),), reach)
    slabs = padded.reshape(windows + WK // WQ - 1, WQ, 2 * atom_width)
    neighbours = jnp.concatenate(
        [slabs[offset : offset + windows] for offset in range(WK // WQ)], axis=1
    )
    key_part = neighbours[:, :, :atom_width].reshape(windows, WK, HA, DA)
    value_part = neighbours[:, :, atom_width:].reshape(windows, WK, HA, DA)
    query_part = atom_queries.reshape(windows, WQ, HA, DA)
    first_atom = lax.axis_index(("row", "col")) * atom_rows
    total_atoms = atom_rows * lax.axis_size(("row", "col"))
    position = (
        first_atom
        + WQ * jnp.arange(windows, dtype=jnp.int32)[:, None]
        + jnp.arange(WK, dtype=jnp.int32)[None, :]
        - reach
    )
    valid = (key_mask == 1) & (position >= 0) & (position < total_atoms)
    scores = jnp.einsum(
        "wqhd,wkhd->whqk", query_part, key_part, preferred_element_type=jnp.float32
    ) * DA ** (-0.5)
    scores = scores + atom_bias.astype(jnp.float32).reshape(windows, WQ, HA, WK).transpose(
        0, 2, 1, 3
    )
    scores = jnp.where(valid[:, None, None, :], scores, MASKED)
    expo = jnp.exp(scores - jnp.max(scores, axis=-1, keepdims=True))
    total = jnp.sum(expo, axis=-1, keepdims=True)
    weights = expo.astype(jnp.bfloat16)
    attended = jnp.einsum(
        "whqk,wkhd->wqhd", weights, value_part, preferred_element_type=jnp.float32
    ) / total.transpose(0, 2, 1, 3)
    gating = jax.nn.sigmoid(product(atom_norm, atom_gate))
    atom_attended = (attended.reshape(atom_rows, atom_width) * gating).astype(jnp.bfloat16)
    atoms_mid = (atoms.astype(jnp.float32) + product(atom_attended, atom_out)).astype(jnp.bfloat16)
    tok_rows, tok_width = tokens.shape
    row_start = lax.axis_index("row") * tok_rows
    atom_local = atom_token - row_start
    selector_rows = (atom_local[:, None] == jnp.arange(tok_rows, dtype=jnp.int32)[None, :]).astype(
        jnp.bfloat16
    )
    row_mid, row_token = (
        lax.all_gather(atoms_mid, "col", axis=0, tiled=True),
        lax.all_gather(atom_token, "col", axis=0, tiled=True),
    )
    row_local = row_token - row_start
    row_select = (jnp.arange(tok_rows, dtype=jnp.int32)[:, None] == row_local[None, :]).astype(
        jnp.bfloat16
    )
    row_features = jax.nn.relu(product(row_mid, pool_weight)).astype(jnp.bfloat16)
    token_sums = product(row_select, row_features)
    token_counts = jnp.sum(row_select.astype(jnp.float32), axis=1)
    tokens_mid = (tokens.astype(jnp.float32) + token_sums / token_counts[:, None]).astype(
        jnp.bfloat16
    )
    token_norm = normalize(tokens_mid.astype(jnp.float32)).astype(jnp.bfloat16)
    token_queries = product(token_norm, token_query).astype(jnp.bfloat16)
    key_count = token_mask.shape[0]
    col_index = lax.axis_index("col")
    every_row = lax.all_gather(token_norm, "row", axis=0, tiled=True)
    key_norm = lax.dynamic_slice_in_dim(every_row, col_index * key_count, key_count, 0)
    token_kv = product(key_norm, token_keyval).astype(jnp.bfloat16)
    head_queries = token_queries.reshape(tok_rows, HT, DT)
    head_keys = token_kv[:, :tok_width].reshape(key_count, HT, DT)
    head_values = token_kv[:, tok_width:].reshape(key_count, HT, DT)
    tok_scores = jnp.einsum(
        "qhd,khd->hqk", head_queries, head_keys, preferred_element_type=jnp.float32
    ) * DT ** (-0.5)
    tok_scores = tok_scores + pair_bias.astype(jnp.float32)
    tok_scores = jnp.where((token_mask == 1)[None, None, :], tok_scores, MASKED)
    local_top = jnp.max(tok_scores, axis=-1)
    tok_exp = jnp.exp(tok_scores - local_top[:, :, None])
    local_total = jnp.sum(tok_exp, axis=-1)
    tok_weights = tok_exp.astype(jnp.bfloat16)
    local_acc = jnp.einsum(
        "hqk,khd->qhd", tok_weights, head_values, preferred_element_type=jnp.float32
    ).reshape(tok_rows, tok_width)
    merged_top, merged_total, merged_acc = combined_all(
        (local_top.T, local_total.T, local_acc), "col", combine_parts
    )
    attended_tok = (merged_acc.reshape(tok_rows, HT, DT) / merged_total[:, :, None]).reshape(
        tok_rows, tok_width
    )
    full_src = finish_rows(attended_tok, token_norm, tokens_mid, token_gate, token_out)
    tokens_new = transition(full_src, trans_gate, trans_up, trans_down)
    token_update = product(tokens_new, back_weight).astype(jnp.bfloat16)
    spread_back = product(selector_rows, token_update)
    atoms_new = (atoms_mid.astype(jnp.float32) + spread_back).astype(jnp.bfloat16)
    return (atoms_new, tokens_new)


def solution(mesh):
    in_specs = (
        P(("row", "col"), None),
        P(("row", "col"), None, None),
        P(("row", "col"), None),
        P(("row", "col")),
        P("row", None),
        P(None, "row", "col"),
        P("col"),
        P(),
        P(),
        P(),
        P(),
        P(),
        P(),
        P(),
        P(),
        P(),
        P(),
        P(),
        P(),
        P(),
    )
    out_specs = (P(("row", "col"), None), P("row", None))
    return jax.shard_map(
        on_device, mesh=mesh, in_specs=in_specs, out_specs=out_specs, check_vma=False
    )
```

profile of v0, /device:TPU:32, one launch (start us, length us, event | category | flops | bytes accessed | tf_op | source)
XLA Modules:
  0.0 491.7 jit_solution(11432116307176533384)
XLA Ops:
  13.9 6.4 %collective-permute-start.1 = (bf16[48,256]{1,0:T(8,128)(2,1)S(1)}, bf16[48,256]{1,0:T(8,128)(2,1)S(1)}, u32[]{:S(2)}, u32[]{:S(2)}) collective-permute-start(bf16[48,256]{1,0:T(8,128)(2,1)S(1)} %get-tuple-element.233), channel_id=1, source_target_pairs={{1,0},{2,1},{3,2},{4,3},{5,4},{6,5},{7,6},{8,7},{9,8},{10,9},{11,1... | collective-permute-start | bytes 73736 | tf_op jit(solution)/shard_map/ppermute | solution.py:26
  26.6 22.6 %all-gather.2 = s32[16,1,256]{2,1,0:T(1,128)S(1)} all-gather(s32[1,1,256]{2,1,0:T(1,128)S(1)} %bitcast.117), channel_id=1, replica_groups=mesh['row'=8,'col'=16] {'col'}, dimensions={0}, use_global_device_ids=true | all-gather | bytes 17408 | tf_op jit(solution)/shard_map/all_gather | solution.py:147
  50.1 20.9 %all-gather.7.cloned.1.call-done = bf16[4096,128]{1,0:T(8,128)(2,1)} async-done(((bf16[256,128]{1,0:T(8,128)(2,1)}), bf16[4096,128]{1,0:T(8,128)(2,1)}) %all-gather.7.cloned.1.call-update) | async-done | bytes 1048592 | tf_op jit(solution)/shard_map/all_gather | solution.py:146
  71.1 6.6 %convert_reduce_fusion.2 = (f32[512]{0:T(512)S(1)}, bf16[512,768]{1,0:T(8,128)(2,1)S(1)}) fusion(f32[512]{0:T(512)S(1)} %convert_reduce_fusion, bf16[4096,128]{1,0:T(8,128)(2,1)} %all-gather.7.cloned.1.call-done, bf16[128,768]{1,0:T(8,128)(2,1)S(1)} %copy-done.9, s32[4096]{0:T(1024)S(1)} %bitcast.116, bf16[512,768]{1,0:T(8,128)(2,1)} %param.26), kind=kOutput, calls=%fused_computation.33 | convolution fusion | flops 4037279232 | bytes 2838528 | tf_op jit(solution)/shard_map/dot_general | solution.py:49
  79.4 6.4 %copy.75 = bf16[16,512,256]{1,2,0:T(8,128)(2,1)} copy(bf16[16,512,256]{2,1,0:T(8,128)(2,1)} %param.27) | data formatting | bytes 8388608 | tf_op args[5]
  91.2 27.5 %all-gather.9.cloned.1.call-done = bf16[4096,768]{1,0:T(8,128)(2,1)} async-done(((bf16[512,768]{1,0:T(8,128)(2,1)}), bf16[4096,768]{1,0:T(8,128)(2,1)}) %all-gather.9.cloned.1.call-update) | async-done | bytes 6291472 | tf_op jit(solution)/shard_map/all_gather | solution.py:163
  126.0 4.9 fusion.83
  137.8 25.1 %all-gather = f32[8192,16]{0,1:T(8,128)S(1)} all-gather(f32[512,16]{0,1:T(8,128)S(1)} %bitcast.106), channel_id=2, replica_groups=mesh['row'=8,'col'=16] {'col'}, dimensions={0}, use_global_device_ids=true | all-gather | bytes 557056 | tf_op jit(solution)/shard_map/all_gather | solution.py:32
  162.9 4.8 fusion.7
  167.7 23.6 %all-gather.1 = f32[8192,16]{0,1:T(8,128)S(1)} all-gather(f32[512,16]{0,1:T(8,128)S(1)} %bitcast.112), channel_id=3, replica_groups=mesh['row'=8,'col'=16] {'col'}, dimensions={0}, use_global_device_ids=true | all-gather | bytes 557056 | tf_op jit(solution)/shard_map/all_gather | solution.py:32
  193.6 102.1 %all-gather.11.cloned.1.call-done = f32[16,512,768]{2,1,0:T(8,128)} async-done(((f32[1,512,768]{2,1,0:T(8,128)}), f32[16,512,768]{2,1,0:T(8,128)}) %all-gather.11.cloned.1.call-update) | async-done | bytes 25165840 | tf_op jit(solution)/shard_map/all_gather | solution.py:32
  301.5 155.7 %while.19 = (s32[]{:T(128)}, f32[512,16]{0,1:T(8,128)S(1)}, f32[512,16]{0,1:T(8,128)S(1)}, f32[512,768]{0,1:T(8,128)}, f32[16,512,16]{1,0,2:T(8,128)}, /*index=5...) while((s32[]{:T(128)}, f32[512,16]{0,1:T(8,128)S(1)}, ...), condition=%wide.region_10.11_spmd, body=%wide.region_9.10_spmd.sunk | while | flops 1228805 | bytes 11468951 | solution.py:38
  308.4 3.5 fusion.109
  318.7 3.5 fusion.109
  329.1 3.5 fusion.109
  339.5 3.5 fusion.109
  349.9 3.5 fusion.109
  360.3 3.5 fusion.109
  370.6 3.5 fusion.109
  381.0 3.5 fusion.109
  391.4 3.5 fusion.109
  464.6 5.2 %convert_reduce_fusion.1 = (f32[512]{0:T(512)S(1)}, bf16[512,768]{1,0:T(8,128)(2,1)}) fusion(bf16[768,768]{1,0:T(8,128)(2,1)} %param.37, f32[512,768]{1,0:T(8,128)} %copy.83, f32[512,768]{1,0:T(8,128)} %copy.84, bf16[768,768]{1,0:T(8,128)(2,1)} %param.36, bf16[512,768]{1,0:T(8,128)(2,1)S(1)} %get-tuple-element.237, f32[512]{0:T(512)S(1)} %add_rsqrt_fusion.1, ...), kind=kOutput, calls=%fused_computation.30 | convolution fusion | flops 1213857280 | bytes 7084032 | tf_op jit(solution)/shard_map/dot_general | solution.py:49
  471.4 4.3 fusion.45
  475.7 7.1 %fusion.22 = bf16[512,768]{1,0:T(8,128)(2,1)} fusion(bf16[512,768]{1,0:T(8,128)(2,1)S(1)} %copy-done.3, bf16[1536,768]{1,0:T(8,128)(2,1)} %param.40, bf16[768,1536]{1,0:T(8,128)(2,1)} %param.39, f32[512,1536]{1,0:T(8,128)} %fusion.45, f32[512]{0:T(512)S(1)} %add_rsqrt_fusion, f32[512]{0:T(512)S(1)} %broadcast_multiply_fusion), kind=kOutput, calls=%fused_computation.43 | convolution fusion | flops 2423390208 | bytes 9441280 | tf_op jit(solution)/shard_map/dot_general | solution.py:49
  (153 shorter events, 178.3 us)
Async XLA Ops:
  7.2 464.2 %copy-start = (bf16[768,1536]{1,0:T(8,128)(2,1)S(1)}, bf16[768,1536]{1,0:T(8,128)(2,1)}, u32[]{:S(2)}) copy-start(bf16[768,1536]{1,0:T(8,128)(2,1)} %param.38) | copy-start | bytes 7077892
  7.2 63.9 %all-gather.7.cloned.1.call-start = ((), (), s32[]{:S(2)}) async-start(), calls=%async_computation | async-start | bytes 1114112 | tf_op jit(solution)/shard_map/all_gather | solution.py:146
  10.5 11.8 %collective-permute-start = (bf16[48,256]{1,0:T(8,128)(2,1)S(1)}, bf16[48,256]{1,0:T(8,128)(2,1)S(1)}, u32[]{:S(2)}, u32[]{:S(2)}) collective-permute-start(bf16[48,256]{1,0:T(8,128)(2,1)S(1)} %get-tuple-element.232), channel_id=1, source_target_pairs={{0,1},{1,2},{2,3},{3,4},{4,5},{5,6},{6,7},{7,8},{8,9},{9,10},{10,1... | collective-permute-start | bytes 73736 | tf_op jit(solution)/shard_map/ppermute | solution.py:25
  13.9 8.4 %collective-permute-start.1 = (bf16[48,256]{1,0:T(8,128)(2,1)S(1)}, bf16[48,256]{1,0:T(8,128)(2,1)S(1)}, u32[]{:S(2)}, u32[]{:S(2)}) collective-permute-start(bf16[48,256]{1,0:T(8,128)(2,1)S(1)} %get-tuple-element.233), channel_id=1, source_target_pairs={{1,0},{2,1},{3,2},{4,3},{5,4},{6,5},{7,6},{8,7},{9,8},{10,9},{11,1... | collective-permute-start | bytes 73736 | tf_op jit(solution)/shard_map/ppermute | solution.py:26
  22.4 1.2 copy-start.6
  23.6 1.0 copy-start.5
  24.6 0.9 copy-start.4
  24.6 0.9 copy-start.11
  24.6 0.9 copy-start.12
  24.9 1.6 copy-start.8
  25.2 45.9 %copy-start.9 = (bf16[128,768]{1,0:T(8,128)(2,1)S(1)}, bf16[128,768]{1,0:T(8,128)(2,1)}, u32[]{:S(2)}) copy-start(bf16[128,768]{1,0:T(8,128)(2,1)} %param.33) | copy-start | bytes 589828
  26.5 92.2 %all-gather.9.cloned.1.call-start = ((), (), s32[]{:S(2)}) async-start(), calls=%async_computation.1 | async-start | bytes 7077888 | tf_op jit(solution)/shard_map/all_gather | solution.py:163
  79.2 216.5 %all-gather.11.cloned.1.call-start = ((), (), s32[]{:S(2)}) async-start(), calls=%async_computation.2 | async-start | bytes 26738688 | tf_op jit(solution)/shard_map/all_gather | solution.py:32
  79.4 6.4 %copy-start.13 = (s32[256]{0:T(256)S(1)}, s32[256]{0:T(256)}, u32[]{:S(2)}) copy-start(s32[256]{0:T(256)} %param.28) | copy-start | bytes 3076
  126.0 4.9 copy-start.2
  130.9 3.8 copy-start.1
  471.3 4.3 copy-start.3
  475.7 7.1 %copy-start.7 = (bf16[256,128]{1,0:T(8,128)(2,1)S(1)}, bf16[256,128]{1,0:T(8,128)(2,1)}, u32[]{:S(2)}) copy-start(bf16[256,128]{1,0:T(8,128)(2,1)} %fusion.34) | copy-start | bytes 196612
  475.7 7.1 %copy-start.10 = (bf16[768,128]{1,0:T(8,128)(2,1)S(1)}, bf16[768,128]{1,0:T(8,128)(2,1)}, u32[]{:S(2)}) copy-start(bf16[768,128]{1,0:T(8,128)(2,1)} %param.41) | copy-start | bytes 589828
Sparse Core Ops, SparseCore 0:
  26.7 44.3 all-gather.6
  79.3 39.3 all-gather.8
  137.9 157.7 all-gather.10
where the time goes:
time: 495 us; the launch traced here: 492 us
  waiting for transfers between devices  151 us (31%)
  local copies, waits for them, and re-layouts  137 us (28%)
  blocking collectives  71.3 us (14%)
  other arithmetic  65.4 us (13%)
  matrix products  43.2 us (9%)
  between operations  14.1 us (3%)
  starting transfers between devices  10.1 us (2%)
    dynamic_slice x45, local copies, waits for them, and re-layouts, hop(): return combine(so_far, jax.tree.map(lambda part: part[k], everything))  102 us
    all_gather x1, waiting for transfers between devices, combined_all(): everything = jax.tree.map(lambda part: lax.all_gather(part, axis), x)  102 us
    add x15, other arithmetic, combine_parts(): acc_both + acc_second.reshape(row_count, head_count, -1) * factor_second[...  52.7 us
    all_gather x2, blocking collectives, combined_all(): everything = jax.tree.map(lambda part: lax.all_gather(part, axis), x)  48.7 us
    dot_general x10, matrix products, product(): return jnp.dot(left, right, preferred_element_type=jnp.float32)  34.4 us
    all_gather x1, waiting for transfers between devices, on_device(): every_row = lax.all_gather(token_norm, 'row', axis=0, tiled=True)  27.5 us
    all_gather x1, blocking collectives, on_device(): lax.all_gather(atom_token, 'col', axis=0, tiled=True)  22.6 us
    all_gather x1, waiting for transfers between devices, on_device(): lax.all_gather(atoms_mid, 'col', axis=0, tiled=True)  20.9 us
  transfers between devices with their start and end apart: 5, of which 3 were waited for; matrix products, arithmetic and copies ran while one was open for 4% of the time, Pallas kernels for 0%

commit v1 on v0

v1 whole, which is shorter than its diff:
```python
import jax
import jax.numpy as jnp
from jax import lax
from jax.experimental import pallas as pl
from jax.experimental.pallas import tpu as pltpu
from jax.sharding import PartitionSpec as P

F32 = jnp.float32
BF16 = jnp.bfloat16
MESH = pl.DeviceIdType.MESH
ROWS, COLS = 8, 16
EPSILON = 1e-05
MASKED = -1000000000.0
HA, DA, WQ, WK = 4, 32, 32, 128
DT = 48
REACH = 48
A = 256
T = 512
K = 256
C = 768
G = 384
OWN = 32
PARTS = 4
H = 128
TOTAL_ATOMS = 32768


def dot(a, b):
    return jnp.dot(a, b, preferred_element_type=F32)


def norm(x):
    mean = jnp.mean(x, axis=-1, keepdims=True)
    d = x - mean
    var = jnp.mean(d * d, axis=-1, keepdims=True)
    return d * lax.rsqrt(var + EPSILON)


def sigmoid(x):
    return 1.0 / (1.0 + jnp.exp(-x))


def iota(shape, dim):
    return lax.broadcasted_iota(jnp.int32, shape, dim)


IN_NAMES = (
    "atoms", "abias", "kmask", "atok", "tokens", "pbias", "tmask", "aq", "akv", "ag", "ao", "pool",
    "tq", "tkv", "tg", "to", "rg", "ru", "rd", "back",
)
EARLY = ("atoms", "akv", "aq", "ag", "kmask", "abias", "ao", "atok", "pool")
LATE = ("tokens", "tg", "tq", "tkv", "tmask", "pbias", "to", "rg", "ru", "rd", "back")
SPANS = tuple(((DT * h) // 128, (DT * h + DT - 1) // 128 - (DT * h) // 128 + 1) for h in range(8))


def split_lse(stat):
    high = stat.astype(BF16).astype(F32)
    rest = stat - high
    middle = rest.astype(BF16).astype(F32)
    third = iota(stat.shape, 1) // 8
    return jnp.where(third == 0, high, jnp.where(third == 1, middle, rest - middle))


def merge(blocks, want_lse):
    l_r, l_c = iota((128, 128), 0), iota((128, 128), 1)
    join = jnp.where((l_r < 24) & (lax.rem(l_r, 8) == lax.rem(l_c, 8)), 1.0, 0.0).astype(BF16)
    s_r, s_c = iota((128, G), 0), iota((128, G), 1)
    spread = jnp.where((s_r < 16) & (lax.rem(s_r, 8) == s_c // DT), 1.0, 0.0).astype(BF16)
    lse = [dot(b[:, G:], join) for b in blocks]
    top = lse[0]
    for l in lse[1:]:
        top = jnp.maximum(top, l)
    wgt = [jnp.exp(l - top) for l in lse]
    total = wgt[0]
    for w in wgt[1:]:
        total = total + w
    inv = 1.0 / total
    first = iota(top.shape, 1) < 8
    out = None
    for w, b in zip(wgt, blocks):
        w = w * inv
        high = w.astype(BF16).astype(F32)
        term = dot(jnp.where(first, high, w - high).astype(BF16), spread) * b[:, :G].astype(F32)
        out = term if out is None else out + term
    if want_lse:
        return jnp.concatenate([out, split_lse(top + jnp.log(total))], axis=1).astype(BF16)
    return out


def kernel(*refs):
    n_in = len(IN_NAMES)
    hbm = dict(zip(IN_NAMES, refs[:n_in]))
    atoms_out, tokens_out = refs[n_in : n_in + 2]
    (
        ext, abias, kmask, tk, tokens, pbias, tmask, aq, akv, ag, ao, pool, tq, tkv, tg, to, rg, ru, rd, back,
        g_mid, feats, acc, selsum, tmid, tnorm, knorm, q_s, kt_s, v_s, snd, rcv, snd2, rcv2, g_new, g_upd,
        in_sem, halo_s, halo_r, tok_s, tok_r, mid_s, mid_r, key_s, key_r,
        one_s, one_r, two_s, two_r, upd_s, upd_r, new_s, new_r, own_sem,
    ) = refs[n_in + 2 :]

    r = lax.axis_index("row")
    c = lax.axis_index("col")
    y, x = c // 4, lax.rem(c, 4)
    z, core = r // 2, lax.rem(r, 2)
    lin = r * COLS + c
    nxt = lax.rem(lin + 1, ROWS * COLS)
    prv = lax.rem(lin + ROWS * COLS - 1, ROWS * COLS)
    nxt_id = (nxt // COLS, lax.rem(nxt, COLS))
    prv_id = (prv // COLS, lax.rem(prv, COLS))
    sibling = (z * 2 + 1 - core, c)

    def remote(src, dst, ss, rs, dev):
        return pltpu.make_async_remote_copy(
            src_ref=src, dst_ref=dst, send_sem=ss, recv_sem=rs, device_id=dev, device_id_type=MESH
        )

    def col_peer(i):
        return lax.rem(c + i, COLS)

    def x_peer(i):
        return y * 4 + lax.rem(x + i, 4)

    def y_peer(i):
        return lax.rem(y + i, 4) * 4 + x

    near = (x_peer, y_peer)

    bar = pltpu.get_barrier_semaphore()
    for dev in (nxt_id, prv_id, sibling, (lax.rem(z + 1, 4) * 2 + core, c), (lax.rem(z + 3, 4) * 2 + core, c)):
        pl.semaphore_signal(bar, inc=1, device_id=dev, device_id_type=MESH)
    for i in range(1, COLS):
        pl.semaphore_signal(bar, inc=1, device_id=(r, col_peer(i)), device_id_type=MESH)

    fetch = {}
    vm = dict(
        atoms=ext.at[pl.ds(REACH, A)], abias=abias, kmask=kmask, atok=tk.at[c], tokens=tokens, pbias=pbias, tmask=tmask,
        aq=aq, akv=akv, ag=ag, ao=ao, pool=pool, tq=tq, tkv=tkv, tg=tg, to=to, rg=rg, ru=ru, rd=rd, back=back,
    )
    for i, name in enumerate(EARLY + LATE):
        fetch[name] = pltpu.make_async_copy(hbm[name], vm[name], in_sem.at[i])
    for name in EARLY:
        fetch[name].start()
    pl.semaphore_wait(bar, 5 + COLS - 1)

    halo = [
        remote(hbm["atoms"].at[pl.ds(A - REACH, REACH)], ext.at[pl.ds(0, REACH)], halo_s.at[0], halo_r.at[0], nxt_id),
        remote(hbm["atoms"].at[pl.ds(0, REACH)], ext.at[pl.ds(REACH + A, REACH)], halo_s.at[1], halo_r.at[1], prv_id),
    ]
    for cp in halo:
        cp.start()

    def tok_copy(i):
        return remote(hbm["atok"], tk.at[c], tok_s.at[col_peer(i)], tok_r.at[c], (r, col_peer(i)))

    for i in range(1, COLS):
        tok_copy(i).start()
    for name in LATE:
        fetch[name].start()

    for name in ("atoms", "akv", "aq", "ag"):
        fetch[name].wait()
    own_f = ext[pl.ds(REACH, A), :].astype(F32)
    own_n = norm(own_f).astype(BF16)
    q_a = dot(own_n, aq[...]).astype(BF16)
    gate_a = sigmoid(dot(own_n, ag[...]))
    kv_own = dot(own_n, akv[...]).astype(BF16)
    fetch["kmask"].wait()
    fetch["abias"].wait()
    p_r = iota((HA * WQ, HA * WQ), 0)
    p_c = iota((HA * WQ, HA * WQ), 1)
    perm = (p_c == lax.rem(p_r, WQ) * HA + p_r // WQ).astype(F32).astype(BF16)
    bias_w = [dot(perm, abias[pl.ds(HA * WQ * w, HA * WQ), :]) for w in range(A // WQ)]
    lane = iota((1, WK), 1)
    head_f = [jnp.where((lane // DA) == h, 1.0, 0.0).astype(F32) for h in range(HA)]
    head_b = [f.astype(BF16) for f in head_f]
    fetch["ao"].wait()

    def mid_at(half, s):
        return g_mid.at[s, pl.ds(H * half, H)]

    def mid_copy(half, s, slot, dev):
        return remote(mid_at(half, s), mid_at(half, s), mid_s.at[half, slot], mid_r.at[half, s], (r, dev))

    def hops(half, send):
        for i in (1, 3, 2):
            send(c, i - 1, near[half](i), None)
        for i in (1, 3, 2):
            send(c, i + 2, near[1 - half](i), None)
        for k, j in enumerate((1, 3, 2)):
            s = near[half](j)
            for i in (1, 3, 2):
                send(s, 3 * k + i + 5, near[1 - half](i), i == 1)

    for half in range(2):
        halo[half].wait_recv()
        edge = norm(ext[pl.ds((REACH + A) * half, REACH), :].astype(F32)).astype(BF16)
        inside = jnp.where(lin == (ROWS * COLS - 1) * half, 0.0, 1.0).astype(F32)
        edge = (dot(edge, akv[...]) * inside).astype(BF16)
        if half == 0:
            kv = jnp.concatenate([edge, kv_own[: H + REACH]], axis=0)
        else:
            kv = jnp.concatenate([kv_own[H - REACH :], edge], axis=0)
        attended = []
        for w in range(4):
            ww = 4 * half + w
            q_w = q_a[WQ * ww : WQ * (ww + 1)]
            q_bd = jnp.concatenate([q_w * head_b[h] for h in range(HA)], axis=0)
            k_w = kv[WQ * w : WQ * w + WK, :WK]
            v_w = kv[WQ * w : WQ * w + WK, WK:]
            s = lax.dot_general(q_bd, k_w, (((1,), (1,)), ((), ())), preferred_element_type=F32)
            s = s * (DA**-0.5) + bias_w[ww]
            pos = lin * A + WQ * ww + lane - REACH
            valid = (kmask[pl.ds(ww, 1), :] == 1) & (pos >= 0) & (pos < TOTAL_ATOMS)
            s = jnp.where(valid, s, MASKED)
            e = jnp.exp(s - jnp.max(s, axis=-1, keepdims=True))
            t = jnp.sum(e, axis=-1, keepdims=True)
            o = dot(e.astype(BF16), v_w) / t
            attended.append(sum(o[WQ * h : WQ * (h + 1)] * head_f[h] for h in range(HA)))
        rows = slice(H * half, H * (half + 1))
        attended = jnp.concatenate(attended, axis=0) * gate_a[rows]
        g_mid[c, rows, :] = (own_f[rows] + dot(attended.astype(BF16), ao[...])).astype(BF16)

        def first(s, slot, dev, arrives):
            if arrives is None:
                mid_copy(half, s, slot, dev).start()

        hops(half, first)

    fetch["pool"].wait()
    fetch["atok"].wait()
    for i in range(1, COLS):
        s = col_peer(i)
        remote(hbm["atok"], tk.at[s], tok_s.at[s], tok_r.at[s], (r, s)).wait_recv()
    for half in range(2):

        def onward(s, slot, dev, arrives):
            if arrives is None:
                return
            if arrives:
                mid_copy(half, s, slot, dev).wait_recv()
            mid_copy(half, s, slot, dev).start()

        hops(half, onward)

    key_off = lax.rem(c, 2) * K

    def step_blocks(step):
        o = lax.rem(step * (step + 1) // 2, 4)
        a = [(lax.rem(y + o, 4) * 4 + b, 0) for b in range(4)]
        return a + [(b * 4 + lax.rem(x + o, 4), 1) for b in range(4)]

    def selector(step, off):
        base = r * T + off
        at = iota((K, H), 0)
        return [
            jnp.where(at == tk[s][:, H * half : H * (half + 1)] - base, 1.0, 0.0).astype(F32)
            for s, half in step_blocks(step)
        ]

    def pool_into(off, step, sel):
        rows = pl.ds(pl.multiple_of(off, K), K)
        count = sel[0]
        for m in sel[1:]:
            count = count + m
        selsum[rows, :] += count
        sel = jnp.concatenate([m.astype(BF16) for m in sel], axis=1)
        acc[rows, :] += dot(sel, feats[pl.ds(pl.multiple_of(step * 1024, 1024), 1024), :])

    acc[...] = jnp.zeros(acc.shape, F32)
    selsum[...] = jnp.zeros(selsum.shape, F32)

    def pool_step(step, carry):
        @pl.when(step > 0)
        def _():
            for s, half in step_blocks(step):
                mid_copy(half, s, 0, s).wait_recv()

        for n, (s, half) in enumerate(step_blocks(step)):
            f = jnp.maximum(dot(g_mid[s, pl.ds(H * half, H), :], pool[...]), 0.0).astype(BF16)
            feats[pl.ds(pl.multiple_of(step * 1024 + H * n, H), H), :] = f
        pool_into(key_off, step, selector(step, key_off))
        return carry

    lax.fori_loop(0, 4, pool_step, 0)
    fetch["tokens"].wait()
    ones = jnp.ones((H, 128), BF16)

    def finish_pool(off):
        def chunk(step, carry):
            rows = pl.ds(pl.multiple_of(off + step * 64, 64), 64)
            inv = 1.0 / dot(selsum[rows, :].astype(BF16), ones)
            inv = jnp.concatenate([inv] * (C // 128), axis=1)
            m = (tokens[rows, :].astype(F32) + acc[rows, :] * inv).astype(BF16)
            tmid[rows, :] = m
            tnorm[rows, :] = norm(m.astype(F32)).astype(BF16)
            return carry

        lax.fori_loop(0, K // 64, chunk, 0)

    finish_pool(key_off)

    z0, core0 = (c // 2) // 2, lax.rem(c // 2, 2)
    away = lax.rem(z - z0 + 4, 4)
    part = K // PARTS
    on_core = core == core0
    is_src = on_core & (away == 0)
    relays = on_core & ((away == 1) | (away == 3))
    shift = jnp.where(away == 3, 2, 0)

    def key_rows(i):
        return pl.ds(pl.multiple_of(i * part, part), part)

    def key_send(i, j):
        dev = sibling if j == 0 else (lax.rem(z + j, 4) * 2 + core, c)
        rows = pl.ds(pl.multiple_of(key_off + i * part, part), part)
        return remote(tnorm.at[rows], knorm.at[key_rows(i)], key_s.at[i, j], key_r.at[i], dev)

    def key_across(i):
        return remote(knorm.at[key_rows(i)], knorm.at[key_rows(i)], key_s.at[i, 0], key_r.at[i], sibling)

    def key_on(i):
        dev = (lax.rem(z + away, 4) * 2 + core, c)
        return remote(knorm.at[key_rows(i)], knorm.at[key_rows(i)], key_s.at[i, 1], key_r.at[i], dev)

    @pl.when(is_src)
    def _():
        for n in range(PARTS):
            key_send(n, 1).start()
            key_send((n + 2) % PARTS, 3).start()
            key_send(n, 0).start()
        knorm[...] = tnorm[pl.ds(pl.multiple_of(key_off, K), K), :]

    def other_step(step, carry):
        pool_into(K - key_off, step, selector(step, K - key_off))
        i = lax.rem(step + shift, PARTS)

        @pl.when(jnp.logical_not(is_src))
        def _():
            key_across(i).wait_recv()

        @pl.when(relays & (step < 2))
        def _():
            key_on(i).start()

        @pl.when(on_core & (away != 0))
        def _():
            key_across(i).start()

        return carry

    lax.fori_loop(0, PARTS, other_step, 0)
    finish_pool(K - key_off)
    fetch["tq"].wait()
    for i in range(4):
        q_s[pl.ds(128 * i, 128), :] = dot(tnorm[pl.ds(128 * i, 128), :], tq[...]).astype(BF16)
    own_rows = pl.ds(pl.multiple_of(c * OWN, OWN), OWN)
    fetch["tg"].wait()
    gate_t = sigmoid(dot(tnorm[own_rows, :], tg[...]))

    fetch["tkv"].wait()
    kt = (dot(knorm[...], tkv[:, :C]) * (DT**-0.5)).T
    row_i = iota((C, 1), 0)
    v_full = dot(knorm[...], tkv[:, C:])
    lane_i = iota((1, C), 1)
    for g in range(2):
        for h in range(8):
            b0, n = SPANS[h]
            lo, hi = G * g + 128 * b0, G * g + 128 * (b0 + n)
            start = G * g + DT * h
            rm = (row_i[lo:hi] >= start) & (row_i[lo:hi] < start + DT)
            kt_s[8 * g + h, pl.ds(0, 128 * n), :] = jnp.where(rm, kt[lo:hi], 0.0).astype(BF16)
            lm = (lane_i[:, lo:hi] >= start) & (lane_i[:, lo:hi] < start + DT)
            v_s[8 * g + h, :, pl.ds(0, 128 * n)] = jnp.where(lm, v_full[:, lo:hi], 0.0).astype(BF16)
    fetch["tmask"].wait()
    fetch["pbias"].wait()

    def one_copy(g, d):
        return remote(snd.at[g, d], rcv.at[g, lax.rem(c // (1 + 3 * g), 4)], one_s.at[g, d],
                      one_r.at[g, lax.rem(c // (1 + 3 * g), 4)], (r, (y * 4 + d) * (1 - g) + (d * 4 + x) * g))

    def attend(step, carry):
        g = lax.rem(step, 2)
        me = lax.rem(c // (1 + 3 * g), 4)
        d = lax.rem(me + 1 + step // 2, 4)
        blocks = [b * (4 - 3 * g) + d * (1 + 3 * g) for b in range(4)]
        rows = [pl.ds(pl.multiple_of(j * OWN, OWN), OWN) for j in blocks]
        live = tmask[...] == 1
        lane8 = lax.rem(iota((128, 128), 1), 8)
        parts = [jnp.zeros((128, 128), F32) for _ in range(3)]
        stat = jnp.zeros((128, 128), F32)
        for h in range(8):
            b0, n = SPANS[h]
            lanes = pl.ds(pl.multiple_of(g * G + 128 * b0, 128), 128 * n)
            qw = jnp.concatenate([q_s[rw, lanes] for rw in rows], axis=0)
            s = dot(qw, kt_s[g * 8 + h, pl.ds(0, 128 * n), :])
            s = s + jnp.concatenate([pbias[g * 8 + h, rw, :] for rw in rows], axis=0).astype(F32)
            s = jnp.where(live, s, MASKED)
            top = jnp.max(s, axis=-1, keepdims=True)
            e = jnp.exp(s - top)
            total = jnp.sum(e, axis=-1, keepdims=True)
            o = dot(e.astype(BF16), v_s[g * 8 + h, :, pl.ds(0, 128 * n)]) * (1.0 / total)
            for b in range(n):
                parts[b0 + b] = parts[b0 + b] + o[:, 128 * b : 128 * (b + 1)]
            stat = jnp.where(lane8 == h, top + jnp.log(total), stat)
        snd[g, d] = jnp.concatenate(parts + [split_lse(stat)], axis=1).astype(BF16)

        @pl.when(d != me)
        def _():
            one_copy(g, d).start()

        return carry

    lax.fori_loop(0, 8, attend, 0)

    mine = (x, y)

    def two_copy(g, d):
        dev = (r, d * 4 + x) if g == 0 else (r, y * 4 + d)
        me = mine[1 - g]
        return remote(snd2.at[g, d], rcv2.at[g, me], two_s.at[g, d], two_r.at[g, me], dev)

    for g in range(2):
        blocks = [snd[g, mine[g]]]
        for i in (1, 3, 2):
            d = lax.rem(mine[g] + i, 4)
            remote(snd.at[g, d], rcv.at[g, d], one_s.at[g, d], one_r.at[g, d], (r, near[g](i))).wait_recv()
            blocks.append(rcv[g, d])
        half_merged = merge(blocks, True)
        for d in range(4):
            snd2[g, d] = half_merged[OWN * d : OWN * (d + 1)]
        for i in (1, 3, 2):
            two_copy(g, lax.rem(mine[1 - g] + i, 4)).start()
    merged = []
    for g in range(2):
        blocks = [snd2[g, mine[1 - g]]]
        for i in (1, 3, 2):
            d = lax.rem(mine[1 - g] + i, 4)
            remote(snd2.at[g, d], rcv2.at[g, d], two_s.at[g, d], two_r.at[g, d], (r, near[1 - g](i))).wait_recv()
            blocks.append(rcv2[g, d])
        merged.append(merge(blocks, False))
    att = jnp.concatenate(merged, axis=1)

    for name in ("to", "rg", "ru", "rd", "back"):
        fetch[name].wait()
    gated = (att * gate_t).astype(BF16)
    t_att = (tmid[own_rows, :].astype(F32) + dot(gated, to[...])).astype(BF16)
    n_att = norm(t_att.astype(F32)).astype(BF16)
    up = dot(n_att, rg[...])
    hid = (up * sigmoid(up) * dot(n_att, ru[...])).astype(BF16)
    t_new = (t_att.astype(F32) + dot(hid, rd[...])).astype(BF16)
    g_new[...] = t_new

    def new_rows(half, s):
        return tokens_out.at[pl.ds(pl.multiple_of(s * OWN + 16 * half, 16), 16)]

    def new_copy(half, s, slot, dev, own):
        src = g_new.at[pl.ds(16 * half, 16)] if own else new_rows(half, s)
        return remote(src, new_rows(half, s), new_s.at[half, slot], new_r.at[half, s], (r, dev))

    for half in range(2):

        def first_new(s, slot, dev, arrives):
            if arrives is None:
                new_copy(half, s, slot, dev, True).start()

        hops(half, first_new)
    own_new = pltpu.make_async_copy(g_new, tokens_out.at[own_rows], own_sem.at[0])
    own_new.start()
    g_upd[c] = dot(t_new, back[...]).astype(BF16)

    def upd_copy(i):
        return remote(g_upd.at[c], g_upd.at[c], upd_s.at[col_peer(i)], upd_r.at[c], (r, col_peer(i)))

    for i in range(1, COLS):
        upd_copy(i).start()
    tok_t = jnp.broadcast_to((tk[c] - r * T).astype(F32), (128, A)).T
    lane_f = iota((A, 128), 1).astype(F32)
    pick = jnp.concatenate(
        [jnp.where(tok_t == lane_f + 128.0 * b, 1.0, 0.0).astype(BF16) for b in range(T // 128)], axis=1
    )
    for half in range(2):

        def onward_new(s, slot, dev, arrives):
            if arrives is None:
                return
            if arrives:
                new_copy(half, s, slot, dev, False).wait_recv()
            new_copy(half, s, slot, dev, False).start()

        hops(half, onward_new)

    for i in range(1, COLS):
        s = col_peer(i)
        remote(g_upd.at[s], g_upd.at[s], upd_s.at[s], upd_r.at[s], (r, s)).wait_recv()
    update = dot(pick, g_upd[...].reshape(T, 128))
    atoms_out[...] = (g_mid[c].astype(F32) + update).astype(BF16)

    for half in range(2):
        for i in (1, 3, 2):
            for j in range(4):
                s = y_peer(i) // 4 * 4 + j if half == 0 else j * 4 + lax.rem(x + i, 4)
                new_copy(half, s, 0, s, False).wait_recv()
    own_new.wait()
    for cp in halo:
        cp.wait_send()
    for i in range(1, COLS):
        tok_copy(i).wait_send()
        upd_copy(i).wait_send()
    for half in range(2):

        def sent(s, slot, dev, arrives):
            mid_copy(half, s, slot, dev).wait_send()
            new_copy(half, s, slot, dev, arrives is None).wait_send()

        hops(half, sent)
    for g in range(2):
        for i in (1, 3, 2):
            one_copy(g, lax.rem(mine[g] + i, 4)).wait_send()
            two_copy(g, lax.rem(mine[1 - g] + i, 4)).wait_send()

    @pl.when(is_src)
    def _():
        for n in range(PARTS):
            for j in (0, 1, 3):
                key_send(n, j).wait_send()

    @pl.when(on_core & (away != 0))
    def _():
        for n in range(PARTS):
            key_across(n).wait_send()

    @pl.when(relays)
    def _():
        for n in range(2):
            key_on(lax.rem(n + shift, PARTS)).wait_send()


def on_device(
    atoms, atom_bias, key_mask, atom_token, tokens, pair_bias, token_mask,
    atom_query, atom_keyval, atom_gate, atom_out, pool_weight,
    token_query, token_keyval, token_gate, token_out, trans_gate, trans_up, trans_down, back_weight,
):
    args = (
        atoms, atom_bias.reshape(A * HA, WK), key_mask, atom_token.reshape(1, A), tokens, pair_bias,
        token_mask.reshape(1, K), atom_query, atom_keyval, atom_gate, atom_out, pool_weight,
        token_query, token_keyval, token_gate, token_out, trans_gate, trans_up, trans_down, back_weight,
    )
    vmem = [pltpu.VMEM(a.shape, a.dtype) for a in args]
    vmem[0] = pltpu.VMEM((A + 2 * REACH, 128), BF16)
    vmem[3] = pltpu.VMEM((COLS, 1, A), jnp.int32)
    dma = pltpu.SemaphoreType.DMA
    scratch = vmem + [
        pltpu.VMEM((COLS, A, 128), BF16),
        pltpu.VMEM((COLS * A, C), BF16),
        pltpu.VMEM((T, C), F32),
        pltpu.VMEM((T, H), F32),
        pltpu.VMEM((T, C), BF16),
        pltpu.VMEM((T, C), BF16),
        pltpu.VMEM((K, C), BF16),
        pltpu.VMEM((T, C), BF16),
        pltpu.VMEM((16, 256, K), BF16),
        pltpu.VMEM((16, K, 256), BF16),
        pltpu.VMEM((2, 4, 4 * OWN, G + 128), BF16),
        pltpu.VMEM((2, 4, 4 * OWN, G + 128), BF16),
        pltpu.VMEM((2, 4, OWN, G + 128), BF16),
        pltpu.VMEM((2, 4, OWN, G + 128), BF16),
        pltpu.VMEM((OWN, C), BF16),
        pltpu.VMEM((COLS, OWN, 128), BF16),
        dma((len(args),)), dma((2,)), dma((2,)),
        dma((COLS,)), dma((COLS,)), dma((2, COLS)), dma((2, COLS)),
        dma((PARTS, 4)), dma((PARTS,)),
        dma((2, 4)), dma((2, 4)), dma((2, 4)), dma((2, 4)),
        dma((COLS,)), dma((COLS,)), dma((2, COLS)), dma((2, COLS)), dma((1,)),
    ]
    return pl.pallas_call(
        kernel,
        out_shape=(jax.ShapeDtypeStruct((A, 128), BF16), jax.ShapeDtypeStruct((T, C), BF16)),
        in_specs=[pl.BlockSpec(memory_space=pl.ANY)] * len(args),
        out_specs=(pl.BlockSpec(memory_space=pltpu.VMEM), pl.BlockSpec(memory_space=pl.ANY)),
        scratch_shapes=scratch,
        compiler_params=pltpu.CompilerParams(
            collective_id=0, has_side_effects=True, vmem_limit_bytes=60 * 1024 * 1024
        ),
        name="block",
    )(*args)


def solution(mesh):
    both = ("row", "col")
    in_specs = (
        P(both, None), P(both, None, None), P(both, None), P(both), P("row", None), P(None, "row", "col"), P("col"),
    ) + (P(),) * 13
    out_specs = (P(both, None), P("row", None))
    return jax.shard_map(on_device, mesh=mesh, in_specs=in_specs, out_specs=out_specs, check_vma=False)
```

time: 495 us -> 76.4 us (0.15)
  waiting for transfers between devices: 151 us -> 0 us
  local copies, waits for them, and re-layouts: 137 us -> 3.54 us
  Pallas kernels: 0 us -> 72 us
  blocking collectives: 71.3 us -> 0 us
  other arithmetic: 65.4 us -> 0 us
  matrix products: 43.2 us -> 0 us
  between operations: 14.1 us -> 0.65 us
  starting transfers between devices: 10.1 us -> 0 us
    all_gather x3 -> x0, waiting for transfers between devices: 151 us -> none  [the longest x1 102 us: combined_all(): everything = jax.tree.map(lambda part: lax.all_gather(part, axis), x)]
    dynamic_slice x45 -> x0, local copies, waits for them, and re-layouts: 102 us -> none  [hop(): return combine(so_far, jax.tree.map(lambda part: part[k], everything))]
    pallas_call x0 -> x1, Pallas kernels: none -> 72 us  [on_device(): pl.pallas_call(kernel, out_shape=(jax.ShapeDtypeStruct((A, 128), BF16), j...]
    all_gather x3 -> x0, blocking collectives: 71.3 us -> none  [the longest x2 48.7 us: combined_all(): everything = jax.tree.map(lambda part: lax.all_gather(part, axis), x)]
    add x31 -> x0, other arithmetic: 53.2 us -> none  [the longest x15 52.7 us: combine_parts(): acc_both + acc_second.reshape(row_count, head_count, -1) * factor_second[...]
    dot_general x14 -> x0, matrix products: 43.2 us -> none  [the longest x10 34.4 us: product(): return jnp.dot(left, right, preferred_element_type=jnp.float32)]
    reduce_sum x7 -> x0, other arithmetic: 10.1 us -> none  [the longest x1 4.83 us: on_device(): local_total = jnp.sum(tok_exp, axis=-1)]
    ppermute x2 -> x0, starting transfers between devices: 9.78 us -> none  [the longest x1 6.38 us: padded_2(): after = lax.ppermute(initial, axis, down)]
  transfers between devices with their start and end apart: 5 -> 0, of which waited for: 3 -> 0; matrix products, arithmetic and copies ran while one was open for 4% -> 0% of each run, Pallas kernels for 0% -> 0%
where the time goes in v1:
time: 76.4 us; the launch traced here: 76.2 us
  Pallas kernels  72 us (94%)
  local copies, waits for them, and re-layouts  3.54 us (5%)
    pallas_call x1, Pallas kernels, on_device(): pl.pallas_call(kernel, out_shape=(jax.ShapeDtypeStruct((A, 128), BF16), j...  72 us
    unnamed x2, local copies, waits for them, and re-layouts  3.54 us

profile of v1, /device:TPU:32, one launch (start us, length us, event | category | flops | bytes accessed | tf_op | source)
XLA Modules:
  0.0 76.2 jit_solution(11727363058051792150)
XLA Ops:
  0.6 72.0 %block.1 = (bf16[256,128]{1,0:T(8,128)(2,1)}, bf16[512,768]{1,0:T(8,128)(2,1)}) custom-call(bf16[256,128]{1,0:T(8,128)(2,1)} %refs_0_.1, bf16[1024,128]{1,0:T(8,128)(2,1)} %bitcast.3, s32[8,128]{1,0:T(8,128)} %refs_2_.1, s32[1,256]{1,0:T(1,128)} %bitcast.4, bf16[512,768]{1,0:T(8,128)(2,1)} %refs_4_.1, bf16[16,512,256]{2,1,0:T(8,128)(2,1)} %refs_5_.1, ...), custom_call_target="tpu_custom_call" | custom-call | tf_op jit(solution)/shard_map/block/pallas_call | solution.py:575
  72.7 1.5 %copy.24 = bf16[256,128]{1,0:T(8,128)(2,1)} copy(bf16[256,128]{1,0:T(8,128)(2,1)} %get-tuple-element.4) | data formatting | bytes 131072
  74.1 2.1 %copy.25 = bf16[512,768]{1,0:T(8,128)(2,1)} copy(bf16[512,768]{1,0:T(8,128)(2,1)} %get-tuple-element.5) | data formatting | bytes 1572864

commit v2 on v1

v2 whole, which is shorter than its diff:
```python
import functools

import jax
import jax.numpy as jnp
from jax import lax
from jax.experimental import pallas as pl
from jax.experimental.pallas import tpu as pltpu
from jax.sharding import PartitionSpec as P

F32 = jnp.float32
BF16 = jnp.bfloat16
MESH = pl.DeviceIdType.MESH
ROWS, COLS = 8, 16
EPSILON = 1e-05
MASKED = -1000000000.0
HA, DA, WQ, WK = 4, 32, 32, 128
DT = 48
REACH = 48
A = 256
T = 512
K = 256
C = 768
G = 384
OWN = 32
H = 128
TOTAL_ATOMS = 32768


def dot(a, b):
    return jnp.dot(a, b, preferred_element_type=F32)


def norm(x):
    mean = jnp.mean(x, axis=-1, keepdims=True)
    d = x - mean
    var = jnp.mean(d * d, axis=-1, keepdims=True)
    return d * lax.rsqrt(var + EPSILON)


def sigmoid(x):
    return 1.0 / (1.0 + jnp.exp(-x))


def iota(shape, dim):
    return lax.broadcasted_iota(jnp.int32, shape, dim)


IN_NAMES = (
    "atoms", "abias", "kmask", "atok", "tokens", "pbias", "tmask", "aq", "akv", "ag", "ao", "pool",
    "tq", "tkv", "tg", "to", "rg", "ru", "rd",
)
EARLY = ("atoms", "akv", "aq", "ag", "kmask", "abias", "ao", "atok", "pool")
LATE = ("tokens", "tg", "tq", "tkv", "tmask", "pbias", "to", "rg", "ru", "rd")
SPANS = tuple(((DT * h) // 128, (DT * h + DT - 1) // 128 - (DT * h) // 128 + 1) for h in range(8))


def split_lse(stat):
    high = stat.astype(BF16).astype(F32)
    rest = stat - high
    middle = rest.astype(BF16).astype(F32)
    third = iota(stat.shape, 1) // 8
    return jnp.where(third == 0, high, jnp.where(third == 1, middle, rest - middle))


def join_lse():
    l_r, l_c = iota((128, 128), 0), iota((128, 128), 1)
    return jnp.where((l_r < 24) & (lax.rem(l_r, 8) == lax.rem(l_c, 8)), 1.0, 0.0).astype(BF16)


def merge(values, lse, want_lse):
    s_r, s_c = iota((128, G), 0), iota((128, G), 1)
    spread = jnp.where((s_r < 16) & (lax.rem(s_r, 8) == s_c // DT), 1.0, 0.0).astype(BF16)
    top = lse[0]
    for l in lse[1:]:
        top = jnp.maximum(top, l)
    wgt = [jnp.exp(l - top) for l in lse]
    total = wgt[0]
    for w in wgt[1:]:
        total = total + w
    inv = 1.0 / total
    first = iota(top.shape, 1) < 8
    out = None
    for w, v in zip(wgt, values):
        w = w * inv
        high = w.astype(BF16).astype(F32)
        term = dot(jnp.where(first, high, w - high).astype(BF16), spread) * v.astype(F32)
        out = term if out is None else out + term
    if want_lse:
        return jnp.concatenate([out, split_lse(top + jnp.log(total))], axis=1).astype(BF16)
    return out


def kernel(*refs):
    n_in = len(IN_NAMES)
    hbm = dict(zip(IN_NAMES, refs[:n_in]))
    mid_out, tokens_out = refs[n_in : n_in + 2]
    (
        ext, abias, kmask, tk, tokens, pbias, tmask, aq, akv, ag, ao, pool, tq, tkv, tg, to, rg, ru, rd,
        g_mid, feats, acc, selsum, tmid, tnorm, knorm, q_s, kt_s, v_s, snd, rcv, snd2, rcv2, g_new,
        in_sem, halo_s, halo_r, tok_s, tok_r, mid_s, mid_r, key_s, key_r,
        one_s, one_r, two_s, two_r, new_s, new_r, own_sem,
    ) = refs[n_in + 2 :]

    r = lax.axis_index("row")
    c = lax.axis_index("col")
    y, x = c // 4, lax.rem(c, 4)
    z, core = r // 2, lax.rem(r, 2)
    lin = r * COLS + c
    nxt = lax.rem(lin + 1, ROWS * COLS)
    prv = lax.rem(lin + ROWS * COLS - 1, ROWS * COLS)
    nxt_id = (nxt // COLS, lax.rem(nxt, COLS))
    prv_id = (prv // COLS, lax.rem(prv, COLS))
    sibling = (z * 2 + 1 - core, c)

    def remote(src, dst, ss, rs, dev):
        return pltpu.make_async_remote_copy(
            src_ref=src, dst_ref=dst, send_sem=ss, recv_sem=rs, device_id=dev, device_id_type=MESH
        )

    def col_peer(i):
        return lax.rem(c + i, COLS)

    def x_peer(i):
        return y * 4 + lax.rem(x + i, 4)

    def y_peer(i):
        return lax.rem(y + i, 4) * 4 + x

    near = (x_peer, y_peer)

    bar = pltpu.get_barrier_semaphore()
    for dev in (nxt_id, prv_id, sibling, (lax.rem(z + 1, 4) * 2 + core, c), (lax.rem(z + 3, 4) * 2 + core, c)):
        pl.semaphore_signal(bar, inc=1, device_id=dev, device_id_type=MESH)
    for i in range(1, COLS):
        pl.semaphore_signal(bar, inc=1, device_id=(r, col_peer(i)), device_id_type=MESH)

    fetch = {}
    vm = dict(
        atoms=ext.at[pl.ds(REACH, A)], abias=abias, kmask=kmask, atok=tk.at[c], tokens=tokens, pbias=pbias, tmask=tmask,
        aq=aq, akv=akv, ag=ag, ao=ao, pool=pool, tq=tq, tkv=tkv, tg=tg, to=to, rg=rg, ru=ru, rd=rd,
    )
    for i, name in enumerate(EARLY + LATE):
        fetch[name] = pltpu.make_async_copy(hbm[name], vm[name], in_sem.at[i])
    for name in EARLY:
        fetch[name].start()

    for name in ("atoms", "akv", "aq", "ag"):
        fetch[name].wait()
    own_f = ext[pl.ds(REACH, A), :].astype(F32)
    own_n = norm(own_f).astype(BF16)
    q_a = dot(own_n, aq[...]).astype(BF16)
    gate_a = sigmoid(dot(own_n, ag[...]))
    kv_own = dot(own_n, akv[...]).astype(BF16)
    fetch["kmask"].wait()
    fetch["abias"].wait()
    p_r = iota((HA * WQ, HA * WQ), 0)
    p_c = iota((HA * WQ, HA * WQ), 1)
    perm = (p_c == lax.rem(p_r, WQ) * HA + p_r // WQ).astype(F32).astype(BF16)
    bias_w = [dot(perm, abias[pl.ds(HA * WQ * w, HA * WQ), :]) for w in range(A // WQ)]
    lane = iota((1, WK), 1)
    head_f = [jnp.where((lane // DA) == h, 1.0, 0.0).astype(F32) for h in range(HA)]
    head_b = [f.astype(BF16) for f in head_f]

    def window(w, kv):
        q_w = q_a[WQ * w : WQ * (w + 1)]
        q_bd = jnp.concatenate([q_w * head_b[h] for h in range(HA)], axis=0)
        s = lax.dot_general(q_bd, kv[:, :WK], (((1,), (1,)), ((), ())), preferred_element_type=F32)
        s = s * (DA**-0.5) + bias_w[w]
        pos = lin * A + WQ * w + lane - REACH
        valid = (kmask[pl.ds(w, 1), :] == 1) & (pos >= 0) & (pos < TOTAL_ATOMS)
        s = jnp.where(valid, s, MASKED)
        e = jnp.exp(s - jnp.max(s, axis=-1, keepdims=True))
        t = jnp.sum(e, axis=-1, keepdims=True)
        o = dot(e.astype(BF16), kv[:, WK:]) / t
        return sum(o[WQ * h : WQ * (h + 1)] * head_f[h] for h in range(HA))

    def mid_of(first, attended):
        rows = slice(first, first + WQ * len(attended))
        gated = (jnp.concatenate(attended, axis=0) * gate_a[rows]).astype(BF16)
        return (own_f[rows] + dot(gated, ao[...])).astype(BF16)

    fetch["ao"].wait()
    g_mid[c, 0:H, :] = mid_of(64, [window(w, kv_own[WQ * w - REACH : WQ * w - REACH + WK]) for w in (2, 3, 4, 5)])
    pl.semaphore_wait(bar, 5 + COLS - 1)

    halo = [
        remote(hbm["atoms"].at[pl.ds(A - REACH, REACH)], ext.at[pl.ds(0, REACH)], halo_s.at[0], halo_r.at[0], nxt_id),
        remote(hbm["atoms"].at[pl.ds(0, REACH)], ext.at[pl.ds(REACH + A, REACH)], halo_s.at[1], halo_r.at[1], prv_id),
    ]
    for cp in halo:
        cp.start()

    def tok_copy(i):
        return remote(hbm["atok"], tk.at[c], tok_s.at[col_peer(i)], tok_r.at[c], (r, col_peer(i)))

    def mid_at(half, s):
        return g_mid.at[s, pl.ds(H * half, H)]

    def mid_copy(half, s, slot, dev):
        return remote(mid_at(half, s), mid_at(half, s), mid_s.at[half, slot], mid_r.at[half, s], (r, dev))

    def hops(half, send):
        for i in (1, 3, 2):
            send(c, i - 1, near[half](i), None)
        for i in (1, 3, 2):
            send(c, i + 2, near[1 - half](i), None)
        for far in (False, True):
            for k, j in enumerate((1, 3, 2)):
                s = near[half](j)
                for i in (2,) if far else (1, 3):
                    send(s, 3 * k + i + 5, near[1 - half](i), i == 1)

    def first(half):
        def send(s, slot, dev, arrives):
            if arrives is None:
                mid_copy(half, s, slot, dev).start()

        hops(half, send)

    first(0)
    for i in range(1, COLS):
        tok_copy(i).start()
    for name in LATE:
        fetch[name].start()
    edges = []
    for side in range(2):
        halo[side].wait_recv()
        edge = norm(ext[pl.ds((REACH + A) * side, REACH), :].astype(F32)).astype(BF16)
        inside = jnp.where(lin == (ROWS * COLS - 1) * side, 0.0, 1.0).astype(F32)
        edges.append((dot(edge, akv[...]) * inside).astype(BF16))
    near_by = jnp.concatenate([kv_own[6 * WQ - REACH :], edges[1]], axis=0)
    g_mid[c, H : H + 64, :] = mid_of(192, [window(6, near_by[:WK]), window(7, near_by[WQ : WQ + WK])])
    near_by = jnp.concatenate([edges[0], kv_own[: WK - WQ + 16]], axis=0)
    g_mid[c, H + 64 :, :] = mid_of(0, [window(0, near_by[:WK]), window(1, near_by[WQ : WQ + WK])])
    first(1)
    mid_out_copies = [
        pltpu.make_async_copy(g_mid.at[c, pl.ds(a, n)], mid_out.at[pl.ds(b, n)], own_sem.at[i])
        for i, (a, b, n) in enumerate(((0, 64, H), (H, 192, 64), (H + 64, 0, 64)))
    ]
    for cp in mid_out_copies:
        cp.start()

    fetch["pool"].wait()
    fetch["atok"].wait()
    for i in range(1, COLS):
        s = col_peer(i)
        remote(hbm["atok"], tk.at[s], tok_s.at[s], tok_r.at[s], (r, s)).wait_recv()
    for half in range(2):

        def onward(s, slot, dev, arrives):
            if arrives is None:
                return
            if arrives:
                mid_copy(half, s, slot, dev).wait_recv()
            mid_copy(half, s, slot, dev).start()

        hops(half, onward)

    key_off = lax.rem(c, 2) * K

    def step_blocks(step):
        o = lax.rem(step * (step + 1) // 2, 4)
        a = [(lax.rem(y + o, 4) * 4 + b, 0) for b in range(4)]
        return a + [(b * 4 + lax.rem(x + o, 4), 1) for b in range(4)]

    def selector(step, off):
        base = r * T + off
        at = iota((K, H), 0)
        sel = []
        for s, half in step_blocks(step):
            turned = pltpu.roll(jnp.broadcast_to(tk[s] - base, (8, A)), 64, 1)
            sel.append(jnp.where(at == turned[0:1, H * (1 - half) : H * (2 - half)], 1.0, 0.0).astype(F32))
        return sel

    def pool_into(off, step, sel):
        rows = pl.ds(pl.multiple_of(off, K), K)
        count = sel[0]
        for m in sel[1:]:
            count = count + m
        selsum[rows, :] += count
        sel = jnp.concatenate([m.astype(BF16) for m in sel], axis=1)
        acc[rows, :] += dot(sel, feats[pl.ds(pl.multiple_of(step * 1024, 1024), 1024), :])

    acc[...] = jnp.zeros(acc.shape, F32)
    selsum[...] = jnp.zeros(selsum.shape, F32)

    def pool_step(step, carry):
        @pl.when(step > 0)
        def _():
            for s, half in step_blocks(step):
                mid_copy(half, s, 0, s).wait_recv()

        for n, (s, half) in enumerate(step_blocks(step)):
            f = jnp.maximum(dot(g_mid[s, pl.ds(H * half, H), :], pool[...]), 0.0).astype(BF16)
            feats[pl.ds(pl.multiple_of(step * 1024 + H * n, H), H), :] = f
        pool_into(key_off, step, selector(step, key_off))
        return carry

    lax.fori_loop(0, 4, pool_step, 0)
    fetch["tokens"].wait()
    ones = jnp.ones((H, 128), BF16)

    def finish_chunk(first):
        rows = pl.ds(pl.multiple_of(first, 128), 128)
        inv = 1.0 / dot(selsum[rows, :].astype(BF16), ones)
        inv = jnp.concatenate([inv] * (C // 128), axis=1)
        m = (tokens[rows, :].astype(F32) + acc[rows, :] * inv).astype(BF16)
        tmid[rows, :] = m
        tnorm[rows, :] = norm(m.astype(F32)).astype(BF16)

    z0, core0 = (c // 2) // 2, lax.rem(c // 2, 2)
    away = lax.rem(z - z0 + 4, 4)
    on_core = core == core0
    is_src = on_core & (away == 0)
    is_sib = jnp.logical_not(on_core) & (away == 0)
    odd = jnp.where(on_core, 0, 1)
    swap = jnp.where(away == 3, 1, 0)
    up, down = (lax.rem(z + 1, 4) * 2 + core, c), (lax.rem(z + 3, 4) * 2 + core, c)
    onward_id = (lax.rem(z + away, 4) * 2 + core, c)

    def key_copy(q, slot, dev):
        rows = knorm.at[pl.ds(pl.multiple_of(q * OWN, OWN), OWN)]
        return remote(rows, rows, key_s.at[q, slot], key_r.at[q], dev)

    def chip_part(n):
        return 2 * lax.rem(n + 2 * swap, 4) + odd

    for pair in range(2):
        finish_chunk(key_off + 128 * pair)

        @pl.when(is_src)
        def _():
            rows = pl.ds(pl.multiple_of(key_off + 128 * pair, 128), 128)
            knorm[pl.ds(128 * pair, 128), :] = tnorm[rows, :]
            q = 4 * pair
            for p in (q + 1, q + 3):
                key_copy(p, 2, sibling).start()
            for p in (q, q + 2):
                key_copy(p, 0, up).start()
            if pair == 1:
                for p in (4, 6, 0, 2):
                    key_copy(p, 1, down).start()
            for p in (q, q + 2):
                key_copy(p, 2, sibling).start()

    @pl.when(is_sib)
    def _():
        for p in (1, 3, 5, 7):
            key_copy(p, 0, up).wait_recv()
            key_copy(p, 0, up).start()
            if p > 4:
                key_copy(p, 1, down).start()
        for p in (1, 3):
            key_copy(p, 1, down).start()

    other_off = K - key_off

    def other_step(step, carry):
        pool_into(other_off, step, selector(step, other_off))

        return carry

    lax.fori_loop(0, 4, other_step, 0)
    own_rows = pl.ds(pl.multiple_of(c * OWN, OWN), OWN)
    for n in range(4):

        @pl.when(away != 0)
        def _():
            key_copy(chip_part(n), 2, sibling).wait_recv()
            key_copy(chip_part(n), 2, sibling).start()

        if n < 2:

            @pl.when((away == 1) | (away == 3))
            def _():
                key_copy(chip_part(n), 0, onward_id).start()

        if n < 2:
            finish_chunk(other_off + 128 * n)
        else:
            if n == 2:
                fetch["tq"].wait()
                fetch["tg"].wait()
            for i in (2 * n - 4, 2 * n - 3):
                q_s[pl.ds(128 * i, 128), :] = dot(tnorm[pl.ds(128 * i, 128), :], tq[...]).astype(BF16)
    gate_t = sigmoid(dot(tnorm[own_rows, :], tg[...]))

    @pl.when(jnp.logical_not(is_src))
    def _():
        for n in range(4):
            q = 2 * n + 1 - odd
            key_copy(q, 2, sibling).wait_recv()

    fetch["tkv"].wait()
    kt = (dot(knorm[...], tkv[:, :C]) * (DT**-0.5)).T
    row_i = iota((C, 1), 0)
    v_full = dot(knorm[...], tkv[:, C:])
    lane_i = iota((1, C), 1)
    for g in range(2):
        for h in range(8):
            b0, n = SPANS[h]
            lo, hi = G * g + 128 * b0, G * g + 128 * (b0 + n)
            start = G * g + DT * h
            rm = (row_i[lo:hi] >= start) & (row_i[lo:hi] < start + DT)
            kt_s[8 * g + h, pl.ds(0, 128 * n), :] = jnp.where(rm, kt[lo:hi], 0.0).astype(BF16)
            lm = (lane_i[:, lo:hi] >= start) & (lane_i[:, lo:hi] < start + DT)
            v_s[8 * g + h, :, pl.ds(0, 128 * n)] = jnp.where(lm, v_full[:, lo:hi], 0.0).astype(BF16)
    fetch["tmask"].wait()
    fetch["pbias"].wait()

    def one_copy(g, d):
        return remote(snd.at[g, d], rcv.at[g, lax.rem(c // (1 + 3 * g), 4)], one_s.at[g, d],
                      one_r.at[g, lax.rem(c // (1 + 3 * g), 4)], (r, (y * 4 + d) * (1 - g) + (d * 4 + x) * g))

    def attend(offsets, g, carry):
        me = lax.rem(c // (1 + 3 * g), 4)
        dests = [lax.rem(me + o, 4) for o in offsets]
        size = 128 * len(dests)
        rows = [
            pl.ds(pl.multiple_of((b * (4 - 3 * g) + d * (1 + 3 * g)) * OWN, OWN), OWN) for d in dests for b in range(4)
        ]
        live = tmask[...] == 1
        lane8 = lax.rem(iota((size, 128), 1), 8)
        parts = [None] * 3
        stat = jnp.zeros((size, 128), F32)
        for h in range(8):
            b0, n = SPANS[h]
            lanes = pl.ds(pl.multiple_of(g * G + 128 * b0, 128), 128 * n)
            qw = jnp.concatenate([q_s[rw, lanes] for rw in rows], axis=0)
            s = dot(qw, kt_s[g * 8 + h, pl.ds(0, 128 * n), :])
            s = s + jnp.concatenate([pbias[g * 8 + h, rw, :] for rw in rows], axis=0).astype(F32)
            s = jnp.where(live, s, MASKED)
            top = jnp.max(s, axis=-1, keepdims=True)
            e = jnp.exp(s - top)
            total = jnp.sum(e, axis=-1, keepdims=True)
            o = dot(e.astype(BF16), v_s[g * 8 + h, :, pl.ds(0, 128 * n)]) * (1.0 / total)
            for b in range(n):
                ob = o[:, 128 * b : 128 * (b + 1)]
                parts[b0 + b] = ob if parts[b0 + b] is None else parts[b0 + b] + ob
            stat = jnp.where(lane8 == h, top + jnp.log(total), stat)
        stat = split_lse(stat)
        for n, d in enumerate(dests):
            for b in range(3):
                snd[g, d, pl.ds(128 * b, 128), :] = parts[b][128 * n : 128 * (n + 1)].astype(BF16)
            snd[g, d, pl.ds(G, 32), :] = stat[128 * n : 128 * (n + 1)].T[:32].astype(BF16)

            if offsets[n] != 0:
                one_copy(g, d).start()

        return carry

    for offsets in ((2,), (1, 3), (0,)):
        lax.fori_loop(0, 2, functools.partial(attend, offsets), 0)

    mine = (x, y)
    join = join_lse()

    def two_copy(g, d):
        dev = (r, d * 4 + x) if g == 0 else (r, y * 4 + d)
        me = mine[1 - g]
        return remote(snd2.at[g, d], rcv2.at[g, me], two_s.at[g, d], two_r.at[g, me], dev)

    for g in range(2):
        blocks = [snd[g, mine[g]]]
        for i in (2, 3, 1):
            d = lax.rem(mine[g] + i, 4)
            remote(snd.at[g, d], rcv.at[g, d], one_s.at[g, d], one_r.at[g, d], (r, near[g](i))).wait_recv()
            blocks.append(rcv[g, d])
        values = [jnp.concatenate([b[128 * k : 128 * (k + 1)] for k in range(3)], axis=1) for b in blocks]
        lse = [
            lax.dot_general(b[G:], join[:32], (((0,), (0,)), ((), ())), preferred_element_type=F32) for b in blocks
        ]
        half_merged = merge(values, lse, True)
        for d in range(4):
            snd2[g, d] = half_merged[OWN * d : OWN * (d + 1)]
        for i in (1, 3, 2):
            two_copy(g, lax.rem(mine[1 - g] + i, 4)).start()
    merged = []
    for g in range(2):
        blocks = [snd2[g, mine[1 - g]]]
        for i in (1, 3, 2):
            d = lax.rem(mine[1 - g] + i, 4)
            remote(snd2.at[g, d], rcv2.at[g, d], two_s.at[g, d], two_r.at[g, d], (r, near[1 - g](i))).wait_recv()
            blocks.append(rcv2[g, d])
        merged.append(merge([b[:, :G] for b in blocks], [dot(b[:, G:], join) for b in blocks], False))
    att = jnp.concatenate(merged, axis=1)

    for name in ("to", "rg", "ru", "rd"):
        fetch[name].wait()
    gated = (att * gate_t).astype(BF16)
    t_att = (tmid[own_rows, :].astype(F32) + dot(gated, to[...])).astype(BF16)
    n_att = norm(t_att.astype(F32)).astype(BF16)
    up = dot(n_att, rg[...])
    hid = (up * sigmoid(up) * dot(n_att, ru[...])).astype(BF16)
    t_new = (t_att.astype(F32) + dot(hid, rd[...])).astype(BF16)
    g_new[own_rows, :] = t_new

    def rows_of(half, s):
        return pl.ds(pl.multiple_of(s * OWN + 16 * half, 16), 16)

    def new_copy(half, s, slot, dev):
        dst = g_new if slot < 3 else tokens_out
        return remote(
            g_new.at[rows_of(half, s)], dst.at[rows_of(half, s)], new_s.at[half, slot], new_r.at[half, s], (r, dev)
        )

    out_copies = [pltpu.make_async_copy(g_new.at[own_rows], tokens_out.at[own_rows], own_sem.at[3])]
    for half in range(2):

        def first_new(s, slot, dev, arrives):
            if arrives is None:
                new_copy(half, s, slot, dev).start()

        hops(half, first_new)
    out_copies[0].start()
    for half in range(2):
        for k, i in enumerate((1, 3, 2)):
            rows = rows_of(half, near[half](i))
            out_copies.append(pltpu.make_async_copy(g_new.at[rows], tokens_out.at[rows], own_sem.at[4 + 3 * half + k]))

    for half in range(2):

        def onward_new(s, slot, dev, arrives):
            if arrives is None:
                return
            if arrives:
                new_copy(half, s, 0, dev).wait_recv()
            new_copy(half, s, slot, dev).start()

        hops(half, onward_new)
    for cp in out_copies[1:]:
        cp.start()

    for half in range(2):
        for i in (1, 3, 2):
            for j in range(4):
                s = y_peer(i) // 4 * 4 + j if half == 0 else j * 4 + lax.rem(x + i, 4)
                new_copy(half, s, 3, s).wait_recv()
    for cp in mid_out_copies + out_copies:
        cp.wait()
    for cp in halo:
        cp.wait_send()
    for i in range(1, COLS):
        tok_copy(i).wait_send()
    for half in range(2):

        def sent(s, slot, dev, arrives):
            mid_copy(half, s, slot, dev).wait_send()
            new_copy(half, s, slot, dev).wait_send()

        hops(half, sent)
    for g in range(2):
        for i in (1, 3, 2):
            one_copy(g, lax.rem(mine[g] + i, 4)).wait_send()
            two_copy(g, lax.rem(mine[1 - g] + i, 4)).wait_send()

    @pl.when(is_src)
    def _():
        for q in range(8):
            key_copy(q, 2, sibling).wait_send()
            if q % 2 == 0:
                key_copy(q, 0, up).wait_send()
                key_copy(q, 1, down).wait_send()

    @pl.when(is_sib)
    def _():
        for q in (1, 3, 5, 7):
            key_copy(q, 0, up).wait_send()
            key_copy(q, 1, down).wait_send()

    @pl.when(away != 0)
    def _():
        for n in range(4):
            key_copy(chip_part(n), 2, sibling).wait_send()

    @pl.when((away == 1) | (away == 3))
    def _():
        for n in (0, 1):
            key_copy(chip_part(n), 0, onward_id).wait_send()


def to_atoms(mid, new, back, atok, atoms_out, tokens_out, mid_v, new_v, back_v, atok_v, in_sem, out_sem):
    n = 4
    rows = [pl.ds(i * (T // n), T // n) for i in range(n)]
    ins = [pltpu.make_async_copy(new.at[w], new_v.at[w], in_sem.at[i]) for i, w in enumerate(rows)]
    small = [
        pltpu.make_async_copy(a, b, in_sem.at[n + i])
        for i, (a, b) in enumerate(((atok, atok_v), (back, back_v), (mid, mid_v)))
    ]
    outs = [pltpu.make_async_copy(new_v.at[w], tokens_out.at[w], out_sem.at[i]) for i, w in enumerate(rows)]
    for cp in ins[:1] + small + ins[1:]:
        cp.start()
    first = lax.axis_index("row") * T
    lane = iota((A, 128), 1).astype(F32)
    ins[0].wait()
    outs[0].start()
    for cp in small:
        cp.wait()
    tok_t = jnp.broadcast_to((atok_v[...] - first).astype(F32), (128, A)).T
    update = None
    for i, w in enumerate(rows):
        if i > 0:
            ins[i].wait()
            outs[i].start()
        pick = jnp.where(tok_t == lane + float(T // n * i), 1.0, 0.0).astype(BF16)
        term = dot(pick, dot(new_v[w, :], back_v[...]).astype(BF16))
        update = term if update is None else update + term
    mid_v[...] = (mid_v[...].astype(F32) + update).astype(BF16)
    last = pltpu.make_async_copy(mid_v, atoms_out, out_sem.at[n])
    last.start()
    for cp in outs + [last]:
        cp.wait()


def on_device(
    atoms, atom_bias, key_mask, atom_token, tokens, pair_bias, token_mask,
    atom_query, atom_keyval, atom_gate, atom_out, pool_weight,
    token_query, token_keyval, token_gate, token_out, trans_gate, trans_up, trans_down, back_weight,
):
    atok = atom_token.reshape(1, A)
    args = (
        atoms, atom_bias.reshape(A * HA, WK), key_mask, atok, tokens, pair_bias,
        token_mask.reshape(1, K), atom_query, atom_keyval, atom_gate, atom_out, pool_weight,
        token_query, token_keyval, token_gate, token_out, trans_gate, trans_up, trans_down,
    )
    vmem = [pltpu.VMEM(a.shape, a.dtype) for a in args]
    vmem[0] = pltpu.VMEM((A + 2 * REACH, 128), BF16)
    vmem[3] = pltpu.VMEM((COLS, 1, A), jnp.int32)
    dma = pltpu.SemaphoreType.DMA
    scratch = vmem + [
        pltpu.VMEM((COLS, A, 128), BF16),
        pltpu.VMEM((COLS * A, C), BF16),
        pltpu.VMEM((T, C), F32),
        pltpu.VMEM((T, H), F32),
        pltpu.VMEM((T, C), BF16),
        pltpu.VMEM((T, C), BF16),
        pltpu.VMEM((K, C), BF16),
        pltpu.VMEM((T, C), BF16),
        pltpu.VMEM((16, 256, K), BF16),
        pltpu.VMEM((16, K, 256), BF16),
        pltpu.VMEM((2, 4, G + 32, 128), BF16),
        pltpu.VMEM((2, 4, G + 32, 128), BF16),
        pltpu.VMEM((2, 4, OWN, G + 128), BF16),
        pltpu.VMEM((2, 4, OWN, G + 128), BF16),
        pltpu.VMEM((T, C), BF16),
        dma((len(args),)), dma((2,)), dma((2,)),
        dma((COLS,)), dma((COLS,)), dma((2, COLS)), dma((2, COLS)),
        dma((8, 3)), dma((8,)),
        dma((2, 4)), dma((2, 4)), dma((2, 4)), dma((2, 4)),
        dma((2, COLS)), dma((2, COLS)), dma((10,)),
    ]
    mid, new = pl.pallas_call(
        kernel,
        out_shape=(jax.ShapeDtypeStruct((A, 128), BF16), jax.ShapeDtypeStruct((T, C), BF16)),
        in_specs=[pl.BlockSpec(memory_space=pl.ANY)] * len(args),
        out_specs=(pl.BlockSpec(memory_space=pl.ANY),) * 2,
        scratch_shapes=scratch,
        compiler_params=pltpu.CompilerParams(
            collective_id=0, has_side_effects=True, vmem_limit_bytes=60 * 1024 * 1024
        ),
        name="block",
    )(*args)
    hbm = pl.BlockSpec(memory_space=pl.ANY)
    return pl.pallas_call(
        to_atoms,
        out_shape=(jax.ShapeDtypeStruct((A, 128), BF16), jax.ShapeDtypeStruct((T, C), BF16)),
        in_specs=[hbm] * 4,
        out_specs=(hbm, hbm),
        scratch_shapes=[
            pltpu.VMEM((A, 128), BF16), pltpu.VMEM((T, C), BF16), pltpu.VMEM((C, 128), BF16), pltpu.VMEM((1, A), jnp.int32),
            dma((7,)), dma((5,)),
        ],
        compiler_params=pltpu.CompilerParams(vmem_limit_bytes=60 * 1024 * 1024),
        name="to_atoms",
    )(mid, new, back_weight, atok)


def solution(mesh):
    both = ("row", "col")
    in_specs = (
        P(both, None), P(both, None, None), P(both, None), P(both), P("row", None), P(None, "row", "col"), P("col"),
    ) + (P(),) * 13
    out_specs = (P(both, None), P("row", None))
    return jax.shard_map(on_device, mesh=mesh, in_specs=in_specs, out_specs=out_specs, check_vma=False)
```

time: 76.4 us -> 69.7 us (0.912)
  local copies, waits for them, and re-layouts: 3.54 us -> 0 us
  Pallas kernels: 72 us -> 68.7 us
    pallas_call x1, Pallas kernels: 72 us -> 65.8 us  [on_device(): pl.pallas_call(kernel, out_shape=(jax.ShapeDtypeStruct((A, 128), BF16), j...]
    unnamed x2 -> x0, local copies, waits for them, and re-layouts: 3.54 us -> none
    pallas_call x0 -> x1, Pallas kernels: none -> 2.88 us  [on_device(): pl.pallas_call(to_atoms, out_shape=(jax.ShapeDtypeStruct((A, 128), BF16),...]
where the time goes in v2:
time: 69.7 us; the launch traced here: 69.5 us
  Pallas kernels  68.7 us (99%)
  between operations  0.81 us (1%)
    pallas_call x1, Pallas kernels, on_device(): pl.pallas_call(kernel, out_shape=(jax.ShapeDtypeStruct((A, 128), BF16), j...  65.8 us
    pallas_call x1, Pallas kernels, on_device(): pl.pallas_call(to_atoms, out_shape=(jax.ShapeDtypeStruct((A, 128), BF16),...  2.88 us

profile of v2, /device:TPU:32, one launch (start us, length us, event | category | flops | bytes accessed | tf_op | source)
XLA Modules:
  0.0 69.5 jit_solution(17318747465510542358)
XLA Ops:
  0.6 65.8 %block.1 = (bf16[256,128]{1,0:T(8,128)(2,1)}, bf16[512,768]{1,0:T(8,128)(2,1)}) custom-call(bf16[256,128]{1,0:T(8,128)(2,1)} %refs_0_.1, bf16[1024,128]{1,0:T(8,128)(2,1)} %bitcast.3, s32[8,128]{1,0:T(8,128)} %refs_2_.1, s32[1,256]{1,0:T(1,128)} %bitcast.4, bf16[512,768]{1,0:T(8,128)(2,1)} %refs_4_.1, bf16[16,512,256]{2,1,0:T(8,128)(2,1)} %refs_5_.1, ...), custom_call_target="tpu_custom_call" | custom-call | tf_op jit(solution)/shard_map/block/pallas_call | solution.py:652
  66.5 2.9 %to_atoms.1 = (bf16[256,128]{1,0:T(8,128)(2,1)}, bf16[512,768]{1,0:T(8,128)(2,1)}) custom-call(bf16[256,128]{1,0:T(8,128)(2,1)} %get-tuple-element.4.mid, bf16[512,768]{1,0:T(8,128)(2,1)} %get-tuple-element.5.new, bf16[768,128]{1,0:T(8,128)(2,1)} %back.1, s32[1,256]{1,0:T(1,128)} %bitcast.5), custom_call_target="tpu_custom_call" | custom-call | tf_op jit(solution)/shard_map/to_atoms/pallas_call | solution.py:664

commit v3 on v2

--- a/solution.py
+++ b/solution.py
@@ -18,6 +18,7 @@
 REACH = 48
 A = 256
 T = 512
+HEAD = 144
 K = 256
 C = 768
 G = 384
@@ -97,7 +98,7 @@
     (
         ext, abias, kmask, tk, tokens, pbias, tmask, aq, akv, ag, ao, pool, tq, tkv, tg, to, rg, ru, rd,
         g_mid, feats, acc, selsum, tmid, tnorm, knorm, q_s, kt_s, v_s, snd, rcv, snd2, rcv2, g_new,
-        in_sem, halo_s, halo_r, tok_s, tok_r, mid_s, mid_r, key_s, key_r,
+        in_sem, halo_s, halo_r, mid_s, mid_r, key_s, key_r,
         one_s, one_r, two_s, two_r, new_s, new_r, own_sem,
     ) = refs[n_in + 2 :]
 
@@ -117,9 +118,6 @@
             src_ref=src, dst_ref=dst, send_sem=ss, recv_sem=rs, device_id=dev, device_id_type=MESH
         )
 
-    def col_peer(i):
-        return lax.rem(c + i, COLS)
-
     def x_peer(i):
         return y * 4 + lax.rem(x + i, 4)
 
@@ -129,14 +127,14 @@
     near = (x_peer, y_peer)
 
     bar = pltpu.get_barrier_semaphore()
-    for dev in (nxt_id, prv_id, sibling, (lax.rem(z + 1, 4) * 2 + core, c), (lax.rem(z + 3, 4) * 2 + core, c)):
+    partners = [nxt_id, prv_id, (lax.rem(z + 1, 4) * 2 + core, c), (lax.rem(z + 3, 4) * 2 + core, c)]
+    partners += [(r, peer(i)) for i in (2, 1, 3) for peer in near] + [sibling]
+    for dev in partners:
         pl.semaphore_signal(bar, inc=1, device_id=dev, device_id_type=MESH)
-    for i in range(1, COLS):
-        pl.semaphore_signal(bar, inc=1, device_id=(r, col_peer(i)), device_id_type=MESH)
 
     fetch = {}
     vm = dict(
-        atoms=ext.at[pl.ds(REACH, A)], abias=abias, kmask=kmask, atok=tk.at[c], tokens=tokens, pbias=pbias, tmask=tmask,
+        atoms=ext.at[pl.ds(REACH, A)], abias=abias, kmask=kmask, atok=tk, tokens=tokens, pbias=pbias, tmask=tmask,
         aq=aq, akv=akv, ag=ag, ao=ao, pool=pool, tq=tq, tkv=tkv, tg=tg, to=to, rg=rg, ru=ru, rd=rd,
     )
     for i, name in enumerate(EARLY + LATE):
@@ -181,47 +179,56 @@
 
     fetch["ao"].wait()
     g_mid[c, 0:H, :] = mid_of(64, [window(w, kv_own[WQ * w - REACH : WQ * w - REACH + WK]) for w in (2, 3, 4, 5)])
-    pl.semaphore_wait(bar, 5 + COLS - 1)
+    fetch["atok"].wait()
+    turned = pltpu.roll(jnp.broadcast_to(tk[...] - r * T, (8, A)), 64, 1)
+    line = iota((16, 128), 0)
+    number = jnp.where(lax.rem(line, 2) == 0, turned[0:1, H:], turned[0:1, :H])
+    number = jnp.where(line < 2, number >> 1, number & 1)
+    g_mid[c, H:HEAD, :] = jnp.where(line < 4, number, 0).astype(F32).astype(BF16)
+    pl.semaphore_wait(bar, len(partners))
 
     halo = [
-        remote(hbm["atoms"].at[pl.ds(A - REACH, REACH)], ext.at[pl.ds(0, REACH)], halo_s.at[0], halo_r.at[0], nxt_id),
-        remote(hbm["atoms"].at[pl.ds(0, REACH)], ext.at[pl.ds(REACH + A, REACH)], halo_s.at[1], halo_r.at[1], prv_id),
+        remote(ext.at[pl.ds(A, REACH)], ext.at[pl.ds(0, REACH)], halo_s.at[0], halo_r.at[0], nxt_id),
+        remote(ext.at[pl.ds(REACH, REACH)], ext.at[pl.ds(REACH + A, REACH)], halo_s.at[1], halo_r.at[1], prv_id),
     ]
     for cp in halo:
         cp.start()
 
-    def tok_copy(i):
-        return remote(hbm["atok"], tk.at[c], tok_s.at[col_peer(i)], tok_r.at[c], (r, col_peer(i)))
-
     def mid_at(half, s):
-        return g_mid.at[s, pl.ds(H * half, H)]
+        return g_mid.at[s, pl.ds(HEAD * half, HEAD - 16 * half)]
 
     def mid_copy(half, s, slot, dev):
         return remote(mid_at(half, s), mid_at(half, s), mid_s.at[half, slot], mid_r.at[half, s], (r, dev))
 
-    def hops(half, send):
-        for i in (1, 3, 2):
-            send(c, i - 1, near[half](i), None)
-        for i in (1, 3, 2):
-            send(c, i + 2, near[1 - half](i), None)
-        for far in (False, True):
-            for k, j in enumerate((1, 3, 2)):
-                s = near[half](j)
-                for i in (2,) if far else (1, 3):
-                    send(s, 3 * k + i + 5, near[1 - half](i), i == 1)
-
-    def first(half):
-        def send(s, slot, dev, arrives):
-            if arrives is None:
-                mid_copy(half, s, slot, dev).start()
-
-        hops(half, send)
-
-    first(0)
-    for i in range(1, COLS):
-        tok_copy(i).start()
+    def own_hops(half, send):
+        for i in (2, 1, 3):
+            send(half, c, i - 1, near[half](i))
+        for i in (2, 1, 3):
+            send(half, c, i + 2, near[1 - half](i))
+
+    def next_hops(half, k, wait, send):
+        s = near[half]((1, 3, 2)[k])
+        if wait is not None:
+            wait(half, s, 0, c).wait_recv()
+        for i in (2, 1, 3):
+            send(half, s, 3 * k + i + 5, near[1 - half](i))
+
+    def all_hops(half, send):
+        own_hops(half, send)
+        for k in range(3):
+            next_hops(half, k, None, send)
+
+    def mid_start(half, s, slot, dev):
+        mid_copy(half, s, slot, dev).start()
+
+    def onward(half):
+        for k in range(3):
+            next_hops(half, k, mid_copy, mid_start)
+
+    own_hops(0, mid_start)
     for name in LATE:
         fetch[name].start()
+    onward(0)
     edges = []
     for side in range(2):
         halo[side].wait_recv()
@@ -229,74 +236,65 @@
         inside = jnp.where(lin == (ROWS * COLS - 1) * side, 0.0, 1.0).astype(F32)
         edges.append((dot(edge, akv[...]) * inside).astype(BF16))
     near_by = jnp.concatenate([kv_own[6 * WQ - REACH :], edges[1]], axis=0)
-    g_mid[c, H : H + 64, :] = mid_of(192, [window(6, near_by[:WK]), window(7, near_by[WQ : WQ + WK])])
+    g_mid[c, HEAD : HEAD + 64, :] = mid_of(192, [window(6, near_by[:WK]), window(7, near_by[WQ : WQ + WK])])
     near_by = jnp.concatenate([edges[0], kv_own[: WK - WQ + 16]], axis=0)
-    g_mid[c, H + 64 :, :] = mid_of(0, [window(0, near_by[:WK]), window(1, near_by[WQ : WQ + WK])])
-    first(1)
+    g_mid[c, HEAD + 64 :, :] = mid_of(0, [window(0, near_by[:WK]), window(1, near_by[WQ : WQ + WK])])
+    own_hops(1, mid_start)
     mid_out_copies = [
         pltpu.make_async_copy(g_mid.at[c, pl.ds(a, n)], mid_out.at[pl.ds(b, n)], own_sem.at[i])
-        for i, (a, b, n) in enumerate(((0, 64, H), (H, 192, 64), (H + 64, 0, 64)))
+        for i, (a, b, n) in enumerate(((0, 64, H), (HEAD, 192, 64), (HEAD + 64, 0, 64)))
     ]
     for cp in mid_out_copies:
         cp.start()
 
     fetch["pool"].wait()
-    fetch["atok"].wait()
-    for i in range(1, COLS):
-        s = col_peer(i)
-        remote(hbm["atok"], tk.at[s], tok_s.at[s], tok_r.at[s], (r, s)).wait_recv()
-    for half in range(2):
-
-        def onward(s, slot, dev, arrives):
-            if arrives is None:
-                return
-            if arrives:
-                mid_copy(half, s, slot, dev).wait_recv()
-            mid_copy(half, s, slot, dev).start()
-
-        hops(half, onward)
 
     key_off = lax.rem(c, 2) * K
 
-    def step_blocks(step):
+    def step_blocks(half, step):
         o = lax.rem(step * (step + 1) // 2, 4)
-        a = [(lax.rem(y + o, 4) * 4 + b, 0) for b in range(4)]
-        return a + [(b * 4 + lax.rem(x + o, 4), 1) for b in range(4)]
-
-    def selector(step, off):
-        base = r * T + off
-        at = iota((K, H), 0)
+        if half == 0:
+            return [lax.rem(y + o, 4) * 4 + b for b in range(4)]
+        return [b * 4 + lax.rem(x + o, 4) for b in range(4)]
+
+    def selector(half, step, off):
+        at = (iota((K, H), 0) + off).astype(F32)
         sel = []
-        for s, half in step_blocks(step):
-            turned = pltpu.roll(jnp.broadcast_to(tk[s] - base, (8, A)), 64, 1)
-            sel.append(jnp.where(at == turned[0:1, H * (1 - half) : H * (2 - half)], 1.0, 0.0).astype(F32))
+        for s in step_blocks(half, step):
+            terms = g_mid[s, H:HEAD, :].astype(F32)
+            number = 2.0 * terms[half : half + 1] + terms[2 + half : 3 + half]
+            sel.append(jnp.where(at == number, 1.0, 0.0).astype(F32))
         return sel
 
-    def pool_into(off, step, sel):
+    def feat_rows(half, step, n):
+        return pl.ds(pl.multiple_of((4 * half + step) * 512, 512), 512 * n)
+
+    def pool_into(off, sel, f):
         rows = pl.ds(pl.multiple_of(off, K), K)
         count = sel[0]
         for m in sel[1:]:
             count = count + m
         selsum[rows, :] += count
-        sel = jnp.concatenate([m.astype(BF16) for m in sel], axis=1)
-        acc[rows, :] += dot(sel, feats[pl.ds(pl.multiple_of(step * 1024, 1024), 1024), :])
+        acc[rows, :] += dot(jnp.concatenate([m.astype(BF16) for m in sel], axis=1), f)
+
+    def pool_step(half, wait, step, carry):
+        blocks = step_blocks(half, step)
+        if wait:
+            for s in blocks:
+                mid_copy(half, s, 0, s).wait_recv()
+        f = jnp.concatenate([g_mid[s, pl.ds(HEAD * half, H), :] for s in blocks], axis=0)
+        f = jnp.maximum(dot(f, pool[...]), 0.0).astype(BF16)
+        feats[feat_rows(half, step, 1), :] = f
+        pool_into(key_off, selector(half, step, key_off), f)
+        return carry
 
     acc[...] = jnp.zeros(acc.shape, F32)
     selsum[...] = jnp.zeros(selsum.shape, F32)
-
-    def pool_step(step, carry):
-        @pl.when(step > 0)
-        def _():
-            for s, half in step_blocks(step):
-                mid_copy(half, s, 0, s).wait_recv()
-
-        for n, (s, half) in enumerate(step_blocks(step)):
-            f = jnp.maximum(dot(g_mid[s, pl.ds(H * half, H), :], pool[...]), 0.0).astype(BF16)
-            feats[pl.ds(pl.multiple_of(step * 1024 + H * n, H), H), :] = f
-        pool_into(key_off, step, selector(step, key_off))
-        return carry
-
-    lax.fori_loop(0, 4, pool_step, 0)
+    for half in range(2):
+        pool_step(half, False, 0, 0)
+        if half == 0:
+            onward(1)
+        lax.fori_loop(1, 4, functools.partial(pool_step, half, True), 0)
     fetch["tokens"].wait()
     ones = jnp.ones((H, 128), BF16)
 
@@ -355,12 +353,13 @@
 
     other_off = K - key_off
 
-    def other_step(step, carry):
-        pool_into(other_off, step, selector(step, other_off))
-
+    def other_step(half, step, carry):
+        sel = selector(half, 2 * step, other_off) + selector(half, 2 * step + 1, other_off)
+        pool_into(other_off, sel, feats[feat_rows(half, 2 * step, 2), :])
         return carry
 
-    lax.fori_loop(0, 4, other_step, 0)
+    for half in range(2):
+        lax.fori_loop(0, 2, functools.partial(other_step, half), 0)
     own_rows = pl.ds(pl.multiple_of(c * OWN, OWN), OWN)
     for n in range(4):
 
@@ -380,10 +379,8 @@
         else:
             if n == 2:
                 fetch["tq"].wait()
-                fetch["tg"].wait()
             for i in (2 * n - 4, 2 * n - 3):
                 q_s[pl.ds(128 * i, 128), :] = dot(tnorm[pl.ds(128 * i, 128), :], tq[...]).astype(BF16)
-    gate_t = sigmoid(dot(tnorm[own_rows, :], tg[...]))
 
     @pl.when(jnp.logical_not(is_src))
     def _():
@@ -452,6 +449,8 @@
     for offsets in ((2,), (1, 3), (0,)):
         lax.fori_loop(0, 2, functools.partial(attend, offsets), 0)
 
+    fetch["tg"].wait()
+    gate_t = sigmoid(dot(tnorm[own_rows, :], tg[...]))
     mine = (x, y)
     join = join_lse()
 
@@ -473,7 +472,7 @@
         half_merged = merge(values, lse, True)
         for d in range(4):
             snd2[g, d] = half_merged[OWN * d : OWN * (d + 1)]
-        for i in (1, 3, 2):
+        for i in (2, 1, 3):
             two_copy(g, lax.rem(mine[1 - g] + i, 4)).start()
     merged = []
     for g in range(2):
@@ -505,29 +504,20 @@
         )
 
     out_copies = [pltpu.make_async_copy(g_new.at[own_rows], tokens_out.at[own_rows], own_sem.at[3])]
+    def new_start(half, s, slot, dev):
+        new_copy(half, s, slot, dev).start()
+
     for half in range(2):
-
-        def first_new(s, slot, dev, arrives):
-            if arrives is None:
-                new_copy(half, s, slot, dev).start()
-
-        hops(half, first_new)
+        own_hops(half, new_start)
     out_copies[0].start()
     for half in range(2):
         for k, i in enumerate((1, 3, 2)):
             rows = rows_of(half, near[half](i))
             out_copies.append(pltpu.make_async_copy(g_new.at[rows], tokens_out.at[rows], own_sem.at[4 + 3 * half + k]))
 
-    for half in range(2):
-
-        def onward_new(s, slot, dev, arrives):
-            if arrives is None:
-                return
-            if arrives:
-                new_copy(half, s, 0, dev).wait_recv()
-            new_copy(half, s, slot, dev).start()
-
-        hops(half, onward_new)
+    for k in range(3):
+        for half in range(2):
+            next_hops(half, k, new_copy, new_start)
     for cp in out_copies[1:]:
         cp.start()
 
@@ -540,15 +530,13 @@
         cp.wait()
     for cp in halo:
         cp.wait_send()
-    for i in range(1, COLS):
-        tok_copy(i).wait_send()
+
+    def sent(half, s, slot, dev):
+        mid_copy(half, s, slot, dev).wait_send()
+        new_copy(half, s, slot, dev).wait_send()
+
     for half in range(2):
-
-        def sent(s, slot, dev, arrives):
-            mid_copy(half, s, slot, dev).wait_send()
-            new_copy(half, s, slot, dev).wait_send()
-
-        hops(half, sent)
+        all_hops(half, sent)
     for g in range(2):
         for i in (1, 3, 2):
             one_copy(g, lax.rem(mine[g] + i, 4)).wait_send()
@@ -580,7 +568,7 @@
 
 
 def to_atoms(mid, new, back, atok, atoms_out, tokens_out, mid_v, new_v, back_v, atok_v, in_sem, out_sem):
-    n = 4
+    n = 8
     rows = [pl.ds(i * (T // n), T // n) for i in range(n)]
     ins = [pltpu.make_async_copy(new.at[w], new_v.at[w], in_sem.at[i]) for i, w in enumerate(rows)]
     small = [
@@ -588,7 +576,7 @@
         for i, (a, b) in enumerate(((atok, atok_v), (back, back_v), (mid, mid_v)))
     ]
     outs = [pltpu.make_async_copy(new_v.at[w], tokens_out.at[w], out_sem.at[i]) for i, w in enumerate(rows)]
-    for cp in ins[:1] + small + ins[1:]:
+    for cp in ins[:2] + small + ins[2:]:
         cp.start()
     first = lax.axis_index("row") * T
     lane = iota((A, 128), 1).astype(F32)
@@ -602,9 +590,11 @@
         if i > 0:
             ins[i].wait()
             outs[i].start()
-        pick = jnp.where(tok_t == lane + float(T // n * i), 1.0, 0.0).astype(BF16)
-        term = dot(pick, dot(new_v[w, :], back_v[...]).astype(BF16))
-        update = term if update is None else update + term
+        if i % 2 == 1:
+            w = pl.ds(T // n * (i - 1), 128)
+            pick = jnp.where(tok_t == lane + float(T // n * (i - 1)), 1.0, 0.0).astype(BF16)
+            term = dot(pick, dot(new_v[w, :], back_v[...]).astype(BF16))
+            update = term if update is None else update + term
     mid_v[...] = (mid_v[...].astype(F32) + update).astype(BF16)
     last = pltpu.make_async_copy(mid_v, atoms_out, out_sem.at[n])
     last.start()
@@ -625,10 +615,9 @@
     )
     vmem = [pltpu.VMEM(a.shape, a.dtype) for a in args]
     vmem[0] = pltpu.VMEM((A + 2 * REACH, 128), BF16)
-    vmem[3] = pltpu.VMEM((COLS, 1, A), jnp.int32)
     dma = pltpu.SemaphoreType.DMA
     scratch = vmem + [
-        pltpu.VMEM((COLS, A, 128), BF16),
+        pltpu.VMEM((COLS, A + 16, 128), BF16),
         pltpu.VMEM((COLS * A, C), BF16),
         pltpu.VMEM((T, C), F32),
         pltpu.VMEM((T, H), F32),
@@ -644,7 +633,7 @@
         pltpu.VMEM((2, 4, OWN, G + 128), BF16),
         pltpu.VMEM((T, C), BF16),
         dma((len(args),)), dma((2,)), dma((2,)),
-        dma((COLS,)), dma((COLS,)), dma((2, COLS)), dma((2, COLS)),
+        dma((2, COLS)), dma((2, COLS)),
         dma((8, 3)), dma((8,)),
         dma((2, 4)), dma((2, 4)), dma((2, 4)), dma((2, 4)),
         dma((2, COLS)), dma((2, COLS)), dma((10,)),
@@ -668,7 +657,7 @@
         out_specs=(hbm, hbm),
         scratch_shapes=[
             pltpu.VMEM((A, 128), BF16), pltpu.VMEM((T, C), BF16), pltpu.VMEM((C, 128), BF16), pltpu.VMEM((1, A), jnp.int32),
-            dma((7,)), dma((5,)),
+            dma((11,)), dma((9,)),
         ],
         compiler_params=pltpu.CompilerParams(vmem_limit_bytes=60 * 1024 * 1024),
         name="to_atoms",

time: 69.7 us -> 67.4 us (0.967)
  Pallas kernels: 68.7 us -> 66.4 us
    pallas_call x1, Pallas kernels: 65.8 us -> 63.4 us  [on_device(): pl.pallas_call(kernel, out_shape=(jax.ShapeDtypeStruct((A, 128), BF16), j...]
where the time goes in v3:
time: 67.4 us; the launch traced here: 67.3 us
  Pallas kernels  66.4 us (99%)
  between operations  0.81 us (1%)
    pallas_call x1, Pallas kernels, on_device(): pl.pallas_call(kernel, out_shape=(jax.ShapeDtypeStruct((A, 128), BF16), j...  63.4 us
    pallas_call x1, Pallas kernels, on_device(): pl.pallas_call(to_atoms, out_shape=(jax.ShapeDtypeStruct((A, 128), BF16),...  3.07 us

profile of v3, /device:TPU:32, one launch (start us, length us, event | category | flops | bytes accessed | tf_op | source)
XLA Modules:
  0.0 67.3 jit_solution(8894900911023998120)
XLA Ops:
  0.6 63.4 %block.1 = (bf16[256,128]{1,0:T(8,128)(2,1)}, bf16[512,768]{1,0:T(8,128)(2,1)}) custom-call(bf16[256,128]{1,0:T(8,128)(2,1)} %refs_0_.1, bf16[1024,128]{1,0:T(8,128)(2,1)} %bitcast.3, s32[8,128]{1,0:T(8,128)} %refs_2_.1, s32[1,256]{1,0:T(1,128)} %bitcast.4, bf16[512,768]{1,0:T(8,128)(2,1)} %refs_4_.1, bf16[16,512,256]{2,1,0:T(8,128)(2,1)} %refs_5_.1, ...), custom_call_target="tpu_custom_call" | custom-call | tf_op jit(solution)/shard_map/block/pallas_call | solution.py:641
  64.0 3.1 %to_atoms.1 = (bf16[256,128]{1,0:T(8,128)(2,1)}, bf16[512,768]{1,0:T(8,128)(2,1)}) custom-call(bf16[256,128]{1,0:T(8,128)(2,1)} %get-tuple-element.4.mid, bf16[512,768]{1,0:T(8,128)(2,1)} %get-tuple-element.5.new, bf16[768,128]{1,0:T(8,128)(2,1)} %back.1, s32[1,256]{1,0:T(1,128)} %bitcast.5), custom_call_target="tpu_custom_call" | custom-call | tf_op jit(solution)/shard_map/to_atoms/pallas_call | solution.py:653

commit v4 on v3

--- a/solution.py
+++ b/solution.py
@@ -18,7 +18,7 @@
 REACH = 48
 A = 256
 T = 512
-HEAD = 144
+PIECES = ((0, 80), (80, 80), (160, 64), (224, 64))
 K = 256
 C = 768
 G = 384
@@ -177,14 +177,22 @@
         gated = (jnp.concatenate(attended, axis=0) * gate_a[rows]).astype(BF16)
         return (own_f[rows] + dot(gated, ao[...])).astype(BF16)
 
+    def put(piece, rows):
+        g_mid[c, PIECES[piece][0] : PIECES[piece][0] + 64, :] = rows
+
     fetch["ao"].wait()
-    g_mid[c, 0:H, :] = mid_of(64, [window(w, kv_own[WQ * w - REACH : WQ * w - REACH + WK]) for w in (2, 3, 4, 5)])
+    inner = mid_of(64, [window(w, kv_own[WQ * w - REACH : WQ * w - REACH + WK]) for w in (2, 3, 4, 5)])
+    put(0, inner[:64])
+    put(1, inner[64:])
     fetch["atok"].wait()
-    turned = pltpu.roll(jnp.broadcast_to(tk[...] - r * T, (8, A)), 64, 1)
-    line = iota((16, 128), 0)
-    number = jnp.where(lax.rem(line, 2) == 0, turned[0:1, H:], turned[0:1, :H])
-    number = jnp.where(line < 2, number >> 1, number & 1)
-    g_mid[c, H:HEAD, :] = jnp.where(line < 4, number, 0).astype(F32).astype(BF16)
+    numbers = jnp.broadcast_to(tk[...] - r * T, (16, A))
+    turned, rest = pltpu.roll(numbers[:, :H], 64, 1), numbers[:, H:]
+    left = iota((16, H), 1) < 64
+    line = iota((16, H), 0)
+    for piece in range(2):
+        number = jnp.where(left, turned, rest) if piece == 0 else jnp.where(left, rest, turned)
+        number = jnp.where(line == 0, number >> 1, jnp.where(line == 1, number & 1, 0))
+        g_mid[c, 64 + 80 * piece : 80 + 80 * piece, :] = number.astype(F32).astype(BF16)
     pl.semaphore_wait(bar, len(partners))
 
     halo = [
@@ -194,41 +202,43 @@
     for cp in halo:
         cp.start()
 
-    def mid_at(half, s):
-        return g_mid.at[s, pl.ds(HEAD * half, HEAD - 16 * half)]
-
-    def mid_copy(half, s, slot, dev):
-        return remote(mid_at(half, s), mid_at(half, s), mid_s.at[half, slot], mid_r.at[half, s], (r, dev))
-
-    def own_hops(half, send):
+    def mid_copy(piece, s, slot, dev):
+        rows = g_mid.at[s, pl.ds(*PIECES[piece])]
+        return remote(rows, rows, mid_s.at[piece, slot], mid_r.at[piece, s], (r, dev))
+
+    def own_hops(piece, send):
+        half = piece % 2
         for i in (2, 1, 3):
-            send(half, c, i - 1, near[half](i))
+            send(piece, c, i - 1, near[half](i))
         for i in (2, 1, 3):
-            send(half, c, i + 2, near[1 - half](i))
-
-    def next_hops(half, k, wait, send):
+            send(piece, c, i + 2, near[1 - half](i))
+
+    def next_hops(piece, k, wait, send):
+        half = piece % 2
         s = near[half]((1, 3, 2)[k])
         if wait is not None:
-            wait(half, s, 0, c).wait_recv()
+            wait(piece, s, 0, c).wait_recv()
         for i in (2, 1, 3):
-            send(half, s, 3 * k + i + 5, near[1 - half](i))
-
-    def all_hops(half, send):
-        own_hops(half, send)
+            send(piece, s, 3 * k + i + 5, near[1 - half](i))
+
+    def all_hops(piece, send):
+        own_hops(piece, send)
         for k in range(3):
-            next_hops(half, k, None, send)
-
-    def mid_start(half, s, slot, dev):
-        mid_copy(half, s, slot, dev).start()
-
-    def onward(half):
+            next_hops(piece, k, None, send)
+
+    def mid_start(piece, s, slot, dev):
+        mid_copy(piece, s, slot, dev).start()
+
+    def onward(pieces):
         for k in range(3):
-            next_hops(half, k, mid_copy, mid_start)
+            for piece in pieces:
+                next_hops(piece, k, mid_copy, mid_start)
 
     own_hops(0, mid_start)
+    own_hops(1, mid_start)
     for name in LATE:
         fetch[name].start()
-    onward(0)
+    onward((0, 1))
     edges = []
     for side in range(2):
         halo[side].wait_recv()
@@ -236,13 +246,14 @@
         inside = jnp.where(lin == (ROWS * COLS - 1) * side, 0.0, 1.0).astype(F32)
         edges.append((dot(edge, akv[...]) * inside).astype(BF16))
     near_by = jnp.concatenate([kv_own[6 * WQ - REACH :], edges[1]], axis=0)
-    g_mid[c, HEAD : HEAD + 64, :] = mid_of(192, [window(6, near_by[:WK]), window(7, near_by[WQ : WQ + WK])])
+    put(2, mid_of(192, [window(6, near_by[:WK]), window(7, near_by[WQ : WQ + WK])]))
+    own_hops(2, mid_start)
     near_by = jnp.concatenate([edges[0], kv_own[: WK - WQ + 16]], axis=0)
-    g_mid[c, HEAD + 64 :, :] = mid_of(0, [window(0, near_by[:WK]), window(1, near_by[WQ : WQ + WK])])
-    own_hops(1, mid_start)
+    put(3, mid_of(0, [window(0, near_by[:WK]), window(1, near_by[WQ : WQ + WK])]))
+    own_hops(3, mid_start)
     mid_out_copies = [
-        pltpu.make_async_copy(g_mid.at[c, pl.ds(a, n)], mid_out.at[pl.ds(b, n)], own_sem.at[i])
-        for i, (a, b, n) in enumerate(((0, 64, H), (HEAD, 192, 64), (HEAD + 64, 0, 64)))
+        pltpu.make_async_copy(g_mid.at[c, pl.ds(PIECES[i][0], 64)], mid_out.at[pl.ds(b, 64)], own_sem.at[i])
+        for i, b in enumerate((64, 128, 192, 0))
     ]
     for cp in mid_out_copies:
         cp.start()
@@ -251,19 +262,25 @@
 
     key_off = lax.rem(c, 2) * K
 
-    def step_blocks(half, step):
+    def step_blocks(step):
         o = lax.rem(step * (step + 1) // 2, 4)
-        if half == 0:
-            return [lax.rem(y + o, 4) * 4 + b for b in range(4)]
-        return [b * 4 + lax.rem(x + o, 4) for b in range(4)]
-
-    def selector(half, step, off):
+        return [lax.rem(y + o, 4) * 4 + b for b in range(4)], [b * 4 + lax.rem(x + o, 4) for b in range(4)]
+
+    def selector(late, step, off):
         at = (iota((K, H), 0) + off).astype(F32)
+        left = iota((8, H), 1) < 64
         sel = []
-        for s in step_blocks(half, step):
-            terms = g_mid[s, H:HEAD, :].astype(F32)
-            number = 2.0 * terms[half : half + 1] + terms[2 + half : 3 + half]
-            sel.append(jnp.where(at == number, 1.0, 0.0).astype(F32))
+        for half, blocks in enumerate(step_blocks(step)):
+            numbers = []
+            for s in blocks:
+                terms = g_mid[s, 64 + 80 * half : 80 + 80 * half, :].astype(F32)
+                numbers.append(jnp.broadcast_to(2.0 * terms[0:1] + terms[1:2], (8, H)))
+            for n in (0, 2):
+                if late:
+                    pair = jnp.where(left, pltpu.roll(numbers[n], 64, 1), numbers[n + 1])
+                else:
+                    pair = jnp.where(left, numbers[n], pltpu.roll(numbers[n + 1], 64, 1))
+                sel.append(jnp.where(at == pair[0:1], 1.0, 0.0).astype(F32))
         return sel
 
     def feat_rows(half, step, n):
@@ -277,24 +294,27 @@
         selsum[rows, :] += count
         acc[rows, :] += dot(jnp.concatenate([m.astype(BF16) for m in sel], axis=1), f)
 
-    def pool_step(half, wait, step, carry):
-        blocks = step_blocks(half, step)
-        if wait:
-            for s in blocks:
-                mid_copy(half, s, 0, s).wait_recv()
-        f = jnp.concatenate([g_mid[s, pl.ds(HEAD * half, H), :] for s in blocks], axis=0)
+    def pool_step(late, wait, step, carry):
+        rows = []
+        for half, blocks in enumerate(step_blocks(step)):
+            piece = 2 * late + half
+            if wait:
+                for s in blocks:
+                    mid_copy(piece, s, 0, s).wait_recv()
+            rows += [g_mid[s, pl.ds(PIECES[piece][0], 64), :] for s in blocks]
+        f = jnp.concatenate(rows, axis=0)
         f = jnp.maximum(dot(f, pool[...]), 0.0).astype(BF16)
-        feats[feat_rows(half, step, 1), :] = f
-        pool_into(key_off, selector(half, step, key_off), f)
+        feats[feat_rows(late, step, 1), :] = f
+        pool_into(key_off, selector(late, step, key_off), f)
         return carry
 
     acc[...] = jnp.zeros(acc.shape, F32)
     selsum[...] = jnp.zeros(selsum.shape, F32)
-    for half in range(2):
-        pool_step(half, False, 0, 0)
-        if half == 0:
-            onward(1)
-        lax.fori_loop(1, 4, functools.partial(pool_step, half, True), 0)
+    for late in range(2):
+        pool_step(late, False, 0, 0)
+        if late == 0:
+            onward((2, 3))
+        lax.fori_loop(1, 4, functools.partial(pool_step, late, True), 0)
     fetch["tokens"].wait()
     ones = jnp.ones((H, 128), BF16)
 
@@ -366,13 +386,16 @@
         @pl.when(away != 0)
         def _():
             key_copy(chip_part(n), 2, sibling).wait_recv()
-            key_copy(chip_part(n), 2, sibling).start()
 
         if n < 2:
 
             @pl.when((away == 1) | (away == 3))
             def _():
                 key_copy(chip_part(n), 0, onward_id).start()
+
+        @pl.when(away != 0)
+        def _():
+            key_copy(chip_part(n), 2, sibling).start()
 
         if n < 2:
             finish_chunk(other_off + 128 * n)
@@ -503,7 +526,7 @@
             g_new.at[rows_of(half, s)], dst.at[rows_of(half, s)], new_s.at[half, slot], new_r.at[half, s], (r, dev)
         )
 
-    out_copies = [pltpu.make_async_copy(g_new.at[own_rows], tokens_out.at[own_rows], own_sem.at[3])]
+    out_copies = [pltpu.make_async_copy(g_new.at[own_rows], tokens_out.at[own_rows], own_sem.at[4])]
     def new_start(half, s, slot, dev):
         new_copy(half, s, slot, dev).start()
 
@@ -513,7 +536,7 @@
     for half in range(2):
         for k, i in enumerate((1, 3, 2)):
             rows = rows_of(half, near[half](i))
-            out_copies.append(pltpu.make_async_copy(g_new.at[rows], tokens_out.at[rows], own_sem.at[4 + 3 * half + k]))
+            out_copies.append(pltpu.make_async_copy(g_new.at[rows], tokens_out.at[rows], own_sem.at[5 + 3 * half + k]))
 
     for k in range(3):
         for half in range(2):
@@ -531,12 +554,10 @@
     for cp in halo:
         cp.wait_send()
 
-    def sent(half, s, slot, dev):
-        mid_copy(half, s, slot, dev).wait_send()
-        new_copy(half, s, slot, dev).wait_send()
-
+    for piece in range(4):
+        all_hops(piece, lambda *a: mid_copy(*a).wait_send())
     for half in range(2):
-        all_hops(half, sent)
+        all_hops(half, lambda *a: new_copy(*a).wait_send())
     for g in range(2):
         for i in (1, 3, 2):
             one_copy(g, lax.rem(mine[g] + i, 4)).wait_send()
@@ -617,7 +638,7 @@
     vmem[0] = pltpu.VMEM((A + 2 * REACH, 128), BF16)
     dma = pltpu.SemaphoreType.DMA
     scratch = vmem + [
-        pltpu.VMEM((COLS, A + 16, 128), BF16),
+        pltpu.VMEM((COLS, A + 32, 128), BF16),
         pltpu.VMEM((COLS * A, C), BF16),
         pltpu.VMEM((T, C), F32),
         pltpu.VMEM((T, H), F32),
@@ -633,10 +654,10 @@
         pltpu.VMEM((2, 4, OWN, G + 128), BF16),
         pltpu.VMEM((T, C), BF16),
         dma((len(args),)), dma((2,)), dma((2,)),
-        dma((2, COLS)), dma((2, COLS)),
+        dma((4, COLS)), dma((4, COLS)),
         dma((8, 3)), dma((8,)),
         dma((2, 4)), dma((2, 4)), dma((2, 4)), dma((2, 4)),
-        dma((2, COLS)), dma((2, COLS)), dma((10,)),
+        dma((2, COLS)), dma((2, COLS)), dma((11,)),
     ]
     mid, new = pl.pallas_call(
         kernel,

time: 67.4 us -> 65.3 us (0.969)
  Pallas kernels: 66.4 us -> 64 us
    pallas_call x1, Pallas kernels: 63.4 us -> 60.9 us  [on_device(): pl.pallas_call(kernel, out_shape=(jax.ShapeDtypeStruct((A, 128), BF16), j...]
where the time goes in v4:
time: 65.3 us; the launch traced here: 64.8 us
  Pallas kernels  64 us (98%)
  between operations  0.81 us (1%)
    pallas_call x1, Pallas kernels, on_device(): pl.pallas_call(kernel, out_shape=(jax.ShapeDtypeStruct((A, 128), BF16), j...  60.9 us
    pallas_call x1, Pallas kernels, on_device(): pl.pallas_call(to_atoms, out_shape=(jax.ShapeDtypeStruct((A, 128), BF16),...  3.08 us

profile of v4, /device:TPU:32, one launch (start us, length us, event | category | flops | bytes accessed | tf_op | source)
XLA Modules:
  0.0 64.8 jit_solution(8346654630228207473)
XLA Ops:
  0.6 60.9 %block.1 = (bf16[256,128]{1,0:T(8,128)(2,1)}, bf16[512,768]{1,0:T(8,128)(2,1)}) custom-call(bf16[256,128]{1,0:T(8,128)(2,1)} %refs_0_.1, bf16[1024,128]{1,0:T(8,128)(2,1)} %bitcast.3, s32[8,128]{1,0:T(8,128)} %refs_2_.1, s32[1,256]{1,0:T(1,128)} %bitcast.4, bf16[512,768]{1,0:T(8,128)(2,1)} %refs_4_.1, bf16[16,512,256]{2,1,0:T(8,128)(2,1)} %refs_5_.1, ...), custom_call_target="tpu_custom_call" | custom-call | tf_op jit(solution)/shard_map/block/pallas_call | solution.py:662
  61.6 3.1 %to_atoms.1 = (bf16[256,128]{1,0:T(8,128)(2,1)}, bf16[512,768]{1,0:T(8,128)(2,1)}) custom-call(bf16[256,128]{1,0:T(8,128)(2,1)} %get-tuple-element.4.mid, bf16[512,768]{1,0:T(8,128)(2,1)} %get-tuple-element.5.new, bf16[768,128]{1,0:T(8,128)(2,1)} %back.1, s32[1,256]{1,0:T(1,128)} %bitcast.5), custom_call_target="tpu_custom_call" | custom-call | tf_op jit(solution)/shard_map/to_atoms/pallas_call | solution.py:674

commit v5 on v4

--- a/solution.py
+++ b/solution.py
@@ -381,6 +381,20 @@
     for half in range(2):
         lax.fori_loop(0, 2, functools.partial(other_step, half), 0)
     own_rows = pl.ds(pl.multiple_of(c * OWN, OWN), OWN)
+    fetch["tq"].wait()
+
+    def queries():
+        for i in range(4):
+            rows = pl.ds(128 * i, 128)
+            q_s[rows, :] = dot(tnorm[rows, :], tq[...]).astype(BF16)
+
+    between = [lambda: finish_chunk(other_off), lambda: finish_chunk(other_off + 128), queries]
+
+    @pl.when(away == 2)
+    def _():
+        for work in between:
+            work()
+
     for n in range(4):
 
         @pl.when(away != 0)
@@ -397,13 +411,8 @@
         def _():
             key_copy(chip_part(n), 2, sibling).start()
 
-        if n < 2:
-            finish_chunk(other_off + 128 * n)
-        else:
-            if n == 2:
-                fetch["tq"].wait()
-            for i in (2 * n - 4, 2 * n - 3):
-                q_s[pl.ds(128 * i, 128), :] = dot(tnorm[pl.ds(128 * i, 128), :], tq[...]).astype(BF16)
+        if n < 3:
+            pl.when(away != 2)(between[n])
 
     @pl.when(jnp.logical_not(is_src))
     def _():
@@ -544,6 +553,40 @@
     for cp in out_copies[1:]:
         cp.start()
 
+    for cp in halo:
+        cp.wait_send()
+
+    for piece in range(4):
+        all_hops(piece, lambda *a: mid_copy(*a).wait_send())
+    for g in range(2):
+        for i in (1, 3, 2):
+            one_copy(g, lax.rem(mine[g] + i, 4)).wait_send()
+            two_copy(g, lax.rem(mine[1 - g] + i, 4)).wait_send()
+
+    @pl.when(is_src)
+    def _():
+        for q in range(8):
+            key_copy(q, 2, sibling).wait_send()
+            if q % 2 == 0:
+                key_copy(q, 0, up).wait_send()
+                key_copy(q, 1, down).wait_send()
+
+    @pl.when(is_sib)
+    def _():
+        for q in (1, 3, 5, 7):
+            key_copy(q, 0, up).wait_send()
+            key_copy(q, 1, down).wait_send()
+
+    @pl.when(away != 0)
+    def _():
+        for n in range(4):
+            key_copy(chip_part(n), 2, sibling).wait_send()
+
+    @pl.when((away == 1) | (away == 3))
+    def _():
+        for n in (0, 1):
+            key_copy(chip_part(n), 0, onward_id).wait_send()
+
     for half in range(2):
         for i in (1, 3, 2):
             for j in range(4):
@@ -551,45 +594,12 @@
                 new_copy(half, s, 3, s).wait_recv()
     for cp in mid_out_copies + out_copies:
         cp.wait()
-    for cp in halo:
-        cp.wait_send()
-
-    for piece in range(4):
-        all_hops(piece, lambda *a: mid_copy(*a).wait_send())
     for half in range(2):
         all_hops(half, lambda *a: new_copy(*a).wait_send())
-    for g in range(2):
-        for i in (1, 3, 2):
-            one_copy(g, lax.rem(mine[g] + i, 4)).wait_send()
-            two_copy(g, lax.rem(mine[1 - g] + i, 4)).wait_send()
-
-    @pl.when(is_src)
-    def _():
-        for q in range(8):
-            key_copy(q, 2, sibling).wait_send()
-            if q % 2 == 0:
-                key_copy(q, 0, up).wait_send()
-                key_copy(q, 1, down).wait_send()
-
-    @pl.when(is_sib)
-    def _():
-        for q in (1, 3, 5, 7):
-            key_copy(q, 0, up).wait_send()
-            key_copy(q, 1, down).wait_send()
-
-    @pl.when(away != 0)
-    def _():
-        for n in range(4):
-            key_copy(chip_part(n), 2, sibling).wait_send()
-
-    @pl.when((away == 1) | (away == 3))
-    def _():
-        for n in (0, 1):
-            key_copy(chip_part(n), 0, onward_id).wait_send()
 
 
 def to_atoms(mid, new, back, atok, atoms_out, tokens_out, mid_v, new_v, back_v, atok_v, in_sem, out_sem):
-    n = 8
+    n = 2
     rows = [pl.ds(i * (T // n), T // n) for i in range(n)]
     ins = [pltpu.make_async_copy(new.at[w], new_v.at[w], in_sem.at[i]) for i, w in enumerate(rows)]
     small = [
@@ -597,7 +607,7 @@
         for i, (a, b) in enumerate(((atok, atok_v), (back, back_v), (mid, mid_v)))
     ]
     outs = [pltpu.make_async_copy(new_v.at[w], tokens_out.at[w], out_sem.at[i]) for i, w in enumerate(rows)]
-    for cp in ins[:2] + small + ins[2:]:
+    for cp in ins[:1] + small + ins[1:]:
         cp.start()
     first = lax.axis_index("row") * T
     lane = iota((A, 128), 1).astype(F32)
@@ -611,10 +621,9 @@
         if i > 0:
             ins[i].wait()
             outs[i].start()
-        if i % 2 == 1:
-            w = pl.ds(T // n * (i - 1), 128)
-            pick = jnp.where(tok_t == lane + float(T // n * (i - 1)), 1.0, 0.0).astype(BF16)
-            term = dot(pick, dot(new_v[w, :], back_v[...]).astype(BF16))
+        for at in range(T // n * i, T // n * (i + 1), 128):
+            pick = jnp.where(tok_t == lane + float(at), 1.0, 0.0).astype(BF16)
+            term = dot(pick, dot(new_v[pl.ds(at, 128), :], back_v[...]).astype(BF16))
             update = term if update is None else update + term
     mid_v[...] = (mid_v[...].astype(F32) + update).astype(BF16)
     last = pltpu.make_async_copy(mid_v, atoms_out, out_sem.at[n])
@@ -678,7 +687,7 @@
         out_specs=(hbm, hbm),
         scratch_shapes=[
             pltpu.VMEM((A, 128), BF16), pltpu.VMEM((T, C), BF16), pltpu.VMEM((C, 128), BF16), pltpu.VMEM((1, A), jnp.int32),
-            dma((11,)), dma((9,)),
+            dma((5,)), dma((3,)),
         ],
         compiler_params=pltpu.CompilerParams(vmem_limit_bytes=60 * 1024 * 1024),
         name="to_atoms",

time: 65.3 us -> 63.3 us (0.969)
  Pallas kernels: 64 us -> 62.3 us
    pallas_call x1, Pallas kernels: 60.9 us -> 59.7 us  [on_device(): pl.pallas_call(kernel, out_shape=(jax.ShapeDtypeStruct((A, 128), BF16), j...]
where the time goes in v5:
time: 63.3 us; the launch traced here: 63.2 us
  Pallas kernels  62.3 us (98%)
  between operations  0.81 us (1%)
    pallas_call x1, Pallas kernels, on_device(): pl.pallas_call(kernel, out_shape=(jax.ShapeDtypeStruct((A, 128), BF16), j...  59.7 us
    pallas_call x1, Pallas kernels, on_device(): pl.pallas_call(to_atoms, out_shape=(jax.ShapeDtypeStruct((A, 128), BF16),...  2.66 us

profile of v5, /device:TPU:32, one launch (start us, length us, event | category | flops | bytes accessed | tf_op | source)
XLA Modules:
  0.0 63.2 jit_solution(4702846336709340543)
XLA Ops:
  0.6 59.7 %block.1 = (bf16[256,128]{1,0:T(8,128)(2,1)}, bf16[512,768]{1,0:T(8,128)(2,1)}) custom-call(bf16[256,128]{1,0:T(8,128)(2,1)} %refs_0_.1, bf16[1024,128]{1,0:T(8,128)(2,1)} %bitcast.3, s32[8,128]{1,0:T(8,128)} %refs_2_.1, s32[1,256]{1,0:T(1,128)} %bitcast.4, bf16[512,768]{1,0:T(8,128)(2,1)} %refs_4_.1, bf16[16,512,256]{2,1,0:T(8,128)(2,1)} %refs_5_.1, ...), custom_call_target="tpu_custom_call" | custom-call | tf_op jit(solution)/shard_map/block/pallas_call | solution.py:671
  60.3 2.7 %to_atoms.1 = (bf16[256,128]{1,0:T(8,128)(2,1)}, bf16[512,768]{1,0:T(8,128)(2,1)}) custom-call(bf16[256,128]{1,0:T(8,128)(2,1)} %get-tuple-element.4.mid, bf16[512,768]{1,0:T(8,128)(2,1)} %get-tuple-element.5.new, bf16[768,128]{1,0:T(8,128)(2,1)} %back.1, s32[1,256]{1,0:T(1,128)} %bitcast.5), custom_call_target="tpu_custom_call" | custom-call | tf_op jit(solution)/shard_map/to_atoms/pallas_call | solution.py:683

commit v6 on v5

--- a/solution.py
+++ b/solution.py
@@ -97,7 +97,7 @@
     mid_out, tokens_out = refs[n_in : n_in + 2]
     (
         ext, abias, kmask, tk, tokens, pbias, tmask, aq, akv, ag, ao, pool, tq, tkv, tg, to, rg, ru, rd,
-        g_mid, feats, acc, selsum, tmid, tnorm, knorm, q_s, kt_s, v_s, snd, rcv, snd2, rcv2, g_new,
+        wk_t, g_mid, feats, acc, selsum, tmid, tnorm, knorm, q_s, kt_s, v_s, snd, rcv, snd2, rcv2, g_new,
         in_sem, halo_s, halo_r, mid_s, mid_r, key_s, key_r,
         one_s, one_r, two_s, two_r, new_s, new_r, own_sem,
     ) = refs[n_in + 2 :]
@@ -258,6 +258,10 @@
     for cp in mid_out_copies:
         cp.start()
 
+    fetch["tkv"].wait()
+    for i in range(C // 128):
+        lanes = slice(128 * i, 128 * (i + 1))
+        wk_t[lanes, :] = tkv[:, lanes].astype(F32).T.astype(BF16)
     fetch["pool"].wait()
 
     key_off = lax.rem(c, 2) * K
@@ -420,8 +424,7 @@
             q = 2 * n + 1 - odd
             key_copy(q, 2, sibling).wait_recv()
 
-    fetch["tkv"].wait()
-    kt = (dot(knorm[...], tkv[:, :C]) * (DT**-0.5)).T
+    kt = lax.dot_general(wk_t[...], knorm[...], (((1,), (1,)), ((), ())), preferred_element_type=F32) * (DT**-0.5)
     row_i = iota((C, 1), 0)
     v_full = dot(knorm[...], tkv[:, C:])
     lane_i = iota((1, C), 1)
@@ -647,6 +650,7 @@
     vmem[0] = pltpu.VMEM((A + 2 * REACH, 128), BF16)
     dma = pltpu.SemaphoreType.DMA
     scratch = vmem + [
+        pltpu.VMEM((C, C), BF16),
         pltpu.VMEM((COLS, A + 32, 128), BF16),
         pltpu.VMEM((COLS * A, C), BF16),
         pltpu.VMEM((T, C), F32),

time: 63.3 us -> 63.4 us (level)
  no operation moved by 1% of the time
where the time goes in v6:
time: 63.4 us; the launch traced here: 63 us
  Pallas kernels  62.2 us (98%)
  between operations  0.81 us (1%)
    pallas_call x1, Pallas kernels, on_device(): pl.pallas_call(kernel, out_shape=(jax.ShapeDtypeStruct((A, 128), BF16), j...  59.6 us
    pallas_call x1, Pallas kernels, on_device(): pl.pallas_call(to_atoms, out_shape=(jax.ShapeDtypeStruct((A, 128), BF16),...  2.67 us

profile of v6, /device:TPU:32, one launch (start us, length us, event | category | flops | bytes accessed | tf_op | source)
XLA Modules:
  0.0 63.0 jit_solution(13273113119233630030)
XLA Ops:
  0.6 59.6 %block.1 = (bf16[256,128]{1,0:T(8,128)(2,1)}, bf16[512,768]{1,0:T(8,128)(2,1)}) custom-call(bf16[256,128]{1,0:T(8,128)(2,1)} %refs_0_.1, bf16[1024,128]{1,0:T(8,128)(2,1)} %bitcast.3, s32[8,128]{1,0:T(8,128)} %refs_2_.1, s32[1,256]{1,0:T(1,128)} %bitcast.4, bf16[512,768]{1,0:T(8,128)(2,1)} %refs_4_.1, bf16[16,512,256]{2,1,0:T(8,128)(2,1)} %refs_5_.1, ...), custom_call_target="tpu_custom_call" | custom-call | tf_op jit(solution)/shard_map/block/pallas_call | solution.py:675
  60.2 2.7 %to_atoms.1 = (bf16[256,128]{1,0:T(8,128)(2,1)}, bf16[512,768]{1,0:T(8,128)(2,1)}) custom-call(bf16[256,128]{1,0:T(8,128)(2,1)} %get-tuple-element.4.mid, bf16[512,768]{1,0:T(8,128)(2,1)} %get-tuple-element.5.new, bf16[768,128]{1,0:T(8,128)(2,1)} %back.1, s32[1,256]{1,0:T(1,128)} %bitcast.5), custom_call_target="tpu_custom_call" | custom-call | tf_op jit(solution)/shard_map/to_atoms/pallas_call | solution.py:687
